TPU v7x, 256 devices: a whole 4x4x8 slice. The times are simulated.
256 devices in a mesh: member: 16 (over y, x), tile: 16 (over z, core).
Axes of the slice: x: 4, y: 4, z: 8, core: 2. Of those that a mesh axis runs over, the one named last changes fastest.
Arguments:
- ensemble_array: bfloat16 [64, 73, 96, 360], P('member', None, 'tile'), may hold values from -60 to 60
- lifting_matrix: bfloat16 [73, 256], replicated, may hold values from -0.75 to 0.75
- spectral_damping_factor: float32 [256, 96], replicated, may hold values from 0.1 to 1.9
- first_layer_matrix: bfloat16 [256, 512], replicated, may hold values from -0.375 to 0.375
- second_layer_matrix: bfloat16 [512, 256], replicated, may hold values from -0.25 to 0.25
- readout_matrix: bfloat16 [256, 73], replicated, may hold values from -0.375 to 0.375
- obs_count: int32 [256], P(('tile', 'member')), may hold values from 1 to 128, as said below
- obs_cell: int32 [256, 128], P(('tile', 'member')), may hold values from 0 to 134
- obs_op: float32 [256, 128, 73], P(('tile', 'member')), may hold values from -0.75 to 0.75
- obs_value: float32 [256, 128], P(('tile', 'member')), may hold values from -12 to 12
- obs_error: float32 [256, 128], P(('tile', 'member')), may hold values from 2 to 32
Outputs:
- analysis: bfloat16 [73, 34560, 64], P(None, ('tile', 'member'))
Inputs may be any that keep to these rules, and one draw needn't show every extreme that they name: Observation slots i < obs_count of a tile are live, the rest ignored; some tile has all 128 live.
All inputs are finite; a program needn't handle non-finite values.
Results may differ from a plain program's by a relative error of at most 0.017.
Values may be sent and summed in bfloat16 or wider, within the bound.
A program may use at most 128 MiB of HBM per device.

v0:
```python
import math

import jax
import jax.numpy as jnp
from jax import lax
from jax.sharding import PartitionSpec as P

MMAX = 96
NS_ITERS = 24


def lon_tables(nlon, mmax):
    lon = jnp.arange(nlon, dtype=jnp.float32)
    wave = jnp.arange(mmax, dtype=jnp.float32)
    phase = jnp.mod(lon[:, None] * wave[None, :], float(nlon))
    angle = 2.0 * math.pi * phase / nlon
    forward = jnp.concatenate([jnp.cos(angle), -jnp.sin(angle)], axis=1)
    factor = jnp.where(wave == 0.0, 1.0, 2.0).astype(jnp.float32) / nlon
    inverse = jnp.concatenate([jnp.cos(angle) * factor, -jnp.sin(angle) * factor], axis=1).T
    return (forward.astype(jnp.bfloat16), inverse.astype(jnp.bfloat16))


def lat_tables(nlat):
    row = jnp.arange(nlat, dtype=jnp.float32)
    phase = jnp.mod((2.0 * row[:, None] + 1.0) * row[None, :], float(4 * nlat))
    basis = jnp.cos(math.pi * phase / (2.0 * nlat))
    factor = jnp.where(row == 0.0, 1.0, 2.0).astype(jnp.float32) / nlat
    forward = (basis * factor[None, :]).T
    return (forward.astype(jnp.bfloat16), basis.astype(jnp.bfloat16))


def tile_terms(patch_index, count, mesh_points, obs_op, value, error):
    latent_dimension = patch_index.shape[1]
    selection_matrix = (
        mesh_points[:, None] == jnp.arange(latent_dimension, dtype=jnp.int32)[None, :]
    ).astype(jnp.bfloat16)
    selected_values = jnp.einsum(
        "zv,rvg->zrg", selection_matrix, patch_index, preferred_element_type=jnp.float32
    )
    counterpart = jnp.einsum("jc,jcn->jn", obs_op, selected_values, precision=lax.Precision.HIGHEST)
    center = jnp.mean(counterpart, axis=1)
    spread = counterpart - center[:, None]
    live = jnp.arange(obs_op.shape[0], dtype=jnp.int32) < count
    weight = jnp.where(live, 1.0 / error, jnp.zeros_like(error))
    gram = jnp.dot((spread * weight[:, None]).T, spread, precision=lax.Precision.HIGHEST)
    innov = jnp.dot(weight * (value - center), spread, precision=lax.Precision.HIGHEST)
    return (gram, innov)


def transform(gram, innov, ensemble_vectors):
    eye = jnp.eye(ensemble_vectors, dtype=jnp.float32)
    system = eye + gram / (ensemble_vectors - 1.0)
    lower = jnp.linalg.cholesky(system)
    mean_weight = jax.scipy.linalg.cho_solve((lower, True), innov) / (ensemble_vectors - 1.0)
    scale = jnp.sqrt(jnp.sum(system * system))

    def newton(step, carry):
        upper, root = carry
        shift = 1.5 * eye - 0.5 * jnp.dot(root, upper, precision=lax.Precision.HIGHEST)
        return (
            jnp.dot(upper, shift, precision=lax.Precision.HIGHEST),
            jnp.dot(shift, root, precision=lax.Precision.HIGHEST),
        )

    upper, root = lax.fori_loop(0, NS_ITERS, newton, (system / scale, eye))
    return root / jnp.sqrt(scale) + mean_weight[:, None]


def update(patch_index, mix):
    base = patch_index.astype(jnp.float32)
    center = jnp.mean(base, axis=2, keepdims=True)
    moved = jnp.einsum("ckf,fn->ckn", base - center, mix, precision=lax.Precision.HIGHEST)
    return (center + moved).astype(jnp.bfloat16)


def shards(
    ensemble_array,
    lifting_matrix,
    spectral_damping_factor,
    first_layer_matrix,
    second_layer_matrix,
    readout_matrix,
    obs_count,
    obs_cell,
    obs_op,
    obs_value,
    obs_error,
):
    predicted_values = jnp.float32
    reduced_precision_source = jnp.bfloat16
    ensemble_vectors, variable_total, lat_rows, nlon = ensemble_array.shape
    bands = lax.axis_size("tile")
    nlat = lat_rows * bands
    latent_dimension = lifting_matrix.shape[1] // bands
    azimuthal_forward, azimuthal_inverse = lon_tables(nlon, MMAX)
    meridional_forward, meridional_inverse = lat_tables(nlat)
    gains = lax.dynamic_slice_in_dim(
        spectral_damping_factor, lax.axis_index("tile") * latent_dimension, latent_dimension, 0
    )
    latent_features = jnp.einsum(
        "zfkn,fx->zxkn", ensemble_array, lifting_matrix, preferred_element_type=predicted_values
    ).astype(reduced_precision_source)
    transformed_slice = jnp.einsum(
        "mepq,qk->mepk",
        lax.all_to_all(latent_features, "tile", split_axis=1, concat_axis=2, tiled=True),
        azimuthal_forward,
        preferred_element_type=predicted_values,
    ).astype(reduced_precision_source)
    harmonic_values = jnp.einsum(
        "fa,dcaz->dcfz",
        meridional_forward,
        transformed_slice,
        preferred_element_type=predicted_values,
    )
    harmonic_amplitude = (harmonic_values * gains[None, :, :, None]).astype(
        reduced_precision_source
    )
    synthesis_slice = jnp.einsum(
        "ay,vgys->vgas",
        meridional_inverse,
        harmonic_amplitude,
        preferred_element_type=predicted_values,
    ).astype(reduced_precision_source)
    spatial_band = jnp.einsum(
        "xvdw,wa->xvda", synthesis_slice, azimuthal_inverse, preferred_element_type=predicted_values
    ).astype(reduced_precision_source)
    physical_space_values = lax.all_to_all(
        spatial_band, "tile", split_axis=2, concat_axis=1, tiled=True
    )
    blended_features = (
        latent_features.astype(predicted_values) + physical_space_values.astype(predicted_values)
    ).astype(reduced_precision_source)
    nested_body = jax.nn.gelu(
        jnp.einsum(
            "kciu,ct->ktiu",
            blended_features,
            first_layer_matrix,
            preferred_element_type=predicted_values,
        )
    ).astype(reduced_precision_source)
    enclosing_body = (
        blended_features.astype(predicted_values)
        + jnp.einsum(
            "auzo,uf->afzo",
            nested_body,
            second_layer_matrix,
            preferred_element_type=predicted_values,
        )
    ).astype(reduced_precision_source)
    lifted_back_values = jnp.einsum(
        "kirb,iz->zrbk", enclosing_body, readout_matrix, preferred_element_type=predicted_values
    )
    prior_ensemble = (
        jnp.transpose(ensemble_array, (1, 2, 3, 0)).astype(predicted_values) + lifted_back_values
    ).astype(reduced_precision_source)
    ensemble_batches = lax.axis_size("member")
    mesh_points = lat_rows * nlon // ensemble_batches
    sorted_lines = prior_ensemble.reshape(
        variable_total, ensemble_batches, mesh_points, ensemble_vectors
    )
    gathered = lax.all_to_all(sorted_lines, "member", split_axis=1, concat_axis=3, tiled=True)
    patch_index = gathered.reshape(variable_total, mesh_points, ensemble_vectors * ensemble_batches)
    gram, innov = tile_terms(
        patch_index, obs_count[0], obs_cell[0], obs_op[0], obs_value[0], obs_error[0]
    )
    gram, innov = lax.psum((gram, innov), ("member", "tile"))
    mix = transform(gram, innov, ensemble_vectors * ensemble_batches)
    return update(patch_index, mix)


def solution(mesh):
    placed = (
        P("member", None, "tile", None),
        P(),
        P(),
        P(),
        P(),
        P(),
        P(("tile", "member")),
        P(("tile", "member"), None),
        P(("tile", "member"), None, None),
        P(("tile", "member"), None),
        P(("tile", "member"), None),
    )
    return jax.shard_map(
        shards,
        mesh=mesh,
        in_specs=placed,
        out_specs=P(None, ("tile", "member"), None),
        check_vma=False,
    )
```

profile of v0, /device:TPU:1, one launch (start us, length us, event | category | flops | bytes accessed | tf_op | source)
XLA Modules:
  0.0 465.6 jit_solution(10890713659938435792)
XLA Ops:
  0.0 4.8 %convert_bitcast_fusion.1 = bf16[4,256,6,360]{1,3,2,0:T(8,128)(2,1)} fusion(bf16[4,73,6,360]{3,0,2,1:T(4,128)(2,1)} %param.13, bf16[73,256]{1,0:T(8,128)(2,1)} %param.14), kind=kOutput, calls=%fused_computation.29 | convolution fusion | flops 325140480 | bytes 5722496 | tf_op jit(solution)/shard_map/zfkn,fx->zxkn/dot_general | solution.py:100
  4.8 8.4 %copy.128 = bf16[4,256,6,360]{3,0,2,1:T(4,128)(2,1)} copy(bf16[4,256,6,360]{1,3,2,0:T(8,128)(2,1)} %convert_bitcast_fusion.1) | data formatting | bytes 8847360 | tf_op jit(solution)/shard_map/convert_element_type | solution.py:102
  13.2 10.1 %all-to-all-start = ((bf16[4,256,6,360]{3,0,2,1:T(4,128)(2,1)}), bf16[4,256,6,360]{3,0,2,1:T(4,128)(2,1)}, u32[]{:S(2)}, u32[]{:S(2)}) async-start(bf16[4,256,6,360]{3,0,2,1:T(4,128)(2,1)} %copy.128), calls=%async_computation | async-start | bytes 9437184 | tf_op jit(solution)/shard_map/all_to_all | solution.py:105
  23.5 0.6 fusion.65
  24.2 0.7 multiply_convert_fusion.2
  24.8 103.3 %all-to-all-done = bf16[4,256,6,360]{3,0,2,1:T(4,128)(2,1)} async-done(((bf16[4,256,6,360]{3,0,2,1:T(4,128)(2,1)}), bf16[4,256,6,360]{3,0,2,1:T(4,128)(2,1)}, u32[]{:S(2)}, u32[]{:S(2)}) %all-to-all-start) | async-done | bytes 4423712 | tf_op jit(solution)/shard_map/all_to_all | solution.py:105
  128.2 3.2 copy.129
  131.4 2.8 copy.130
  134.1 7.9 %fusion.30 = f32[4,16,192,96]{3,2,1,0:T(8,128)} fusion(bf16[4,16,96,360]{3,1,2,0:T(8,128)(2,1)} %bitcast.165, bf16[360,96]{0,1:T(8,128)(2,1)S(1)} %get-tuple-element.70, bf16[360,96]{0,1:T(8,128)(2,1)S(1)} %get-tuple-element.69, f32[96]{0:T(128)S(1)} %get-tuple-element.72, f32[96]{0:T(128)S(1)} %get-tuple-element.71), kind=kOutput, calls=%fused_computation.36 | convolution fusion | flops 1077387264 | bytes 9281280 | tf_op jit(solution)/shard_map/fa,dcaz->dcfz/dot_general | solution.py:109
  142.0 7.9 %fusion.33 = bf16[4,16,96,360]{3,2,1,0:T(8,128)(2,1)} fusion(f32[4,16,192,96]{3,2,1,0:T(8,128)} %fusion.30, f32[16,96]{1,0:T(8,128)S(1)} %copy.133, bf16[360,96]{0,1:T(8,128)(2,1)S(1)} %get-tuple-element.68, bf16[360,96]{0,1:T(8,128)(2,1)S(1)} %get-tuple-element.67, f32[96]{0:T(128)S(1)} %get-tuple-element.71), kind=kOutput, calls=%fused_computation.40 | convolution fusion | flops 1081949184 | bytes 9287040 | tf_op jit(solution)/shard_map/xvdw,wa->xvda/dot_general | solution.py:124
  150.0 4.1 copy.135
  154.0 112.5 %all_to_all.42 = bf16[4,16,96,360]{3,1,0,2:T(8,128)(2,1)S(1)} all-to-all(bf16[4,16,96,360]{3,1,0,2:T(8,128)(2,1)S(1)} %copy.135), channel_id=1, replica_groups=mesh['member'=16,'tile'=16] {'tile'}, dimensions={2} | all-to-all | bytes 8847360 | tf_op jit(solution)/shard_map/all_to_all | solution.py:127
  266.5 0.5 copy.136
  267.0 1.3 convert_bitcast_fusion
  268.3 4.9 %copy.137 = f32[4,16,16,6,360]{4,2,1,3,0:T(8,128)} copy(f32[4,16,16,6,360]{4,2,3,1,0:T(8,128)S(1)} %convert_bitcast_fusion) | data formatting | bytes 17694720 | tf_op jit(solution)/shard_map/convert_element_type | solution.py:131
  273.1 9.4 %copy.138 = f32[4,256,6,360]{1,3,2,0:T(8,128)} copy(f32[4,256,6,360]{3,1,2,0:T(8,128)} %bitcast.163) | data formatting | bytes 17694720 | tf_op jit(solution)/shard_map/convert_element_type | solution.py:131
  282.6 12.2 %fusion.12 = f32[4,6,360,256]{3,2,1,0:T(8,128)} fusion(bf16[512,256]{1,0:T(8,128)(2,1)S(1)} %copy-done, bf16[256,512]{1,0:T(8,128)(2,1)S(1)} %copy-done.8, f32[4,256,6,360]{1,3,2,0:T(8,128)} %copy.138, bf16[4,256,6,360]{1,3,2,0:T(8,128)(2,1)} %convert_bitcast_fusion.1), kind=kOutput, calls=%fused_computation.18 | convolution fusion | flops 4576296960 | bytes 22642688 | tf_op jit(solution)/shard_map/auzo,uf->afzo/dot_general | solution.py:143
  294.8 9.1 %fusion.32 = bf16[73,6,360,4]{2,0,1,3:T(8,128)(2,1)S(1)} fusion(f32[4,6,360,256]{3,2,1,0:T(8,128)} %fusion.12, bf16[4,73,6,360]{3,0,2,1:T(4,128)(2,1)S(1)} %copy-done.2, bf16[256,73]{0,1:T(8,128)(2,1)S(1)} %copy-done.4, f32[4,256,6,360]{1,3,2,0:T(8,128)} %copy.138, bf16[4,256,6,360]{1,3,2,0:T(8,128)(2,1)} %convert_bitcast_fusion.1), kind=kOutput, calls=%fused_computation.39 | convolution fusion | flops 338091840 | bytes 24678656 | tf_op jit(solution)/shard_map/kirb,iz->zrbk/dot_general | solution.py:150
  303.9 3.3 copy.164
  307.2 6.8 %all-to-all-start.2 = ((bf16[73,16,135,4]{0,3,2,1:T(4,128)(2,1)}), bf16[73,16,135,4]{0,3,2,1:T(4,128)(2,1)S(1)}, u32[]{:S(2)}, u32[]{:S(2)}) async-start(bf16[73,16,135,4]{0,3,2,1:T(4,128)(2,1)} %bitcast.167), calls=%async_computation.2 | async-start | bytes 4423680 | tf_op jit(solution)/shard_map/all_to_all | solution.py:161
  314.7 34.6 %all-to-all-done.2 = bf16[73,16,135,4]{0,3,2,1:T(4,128)(2,1)S(1)} async-done(((bf16[73,16,135,4]{0,3,2,1:T(4,128)(2,1)}), bf16[73,16,135,4]{0,3,2,1:T(4,128)(2,1)S(1)}, u32[]{:S(2)}, u32[]{:S(2)}) %all-to-all-start.2) | async-done | bytes 1261472 | tf_op jit(solution)/shard_map/all_to_all | solution.py:161
  349.2 0.7 copy.188
  349.9 1.4 copy.144
  351.4 1.4 copy-done.3
  352.7 1.4 multiply_reduce_fusion
  354.1 0.2 fusion.77
  354.5 73.1 %all-reduce = (f32[64,64]{1,0:T(8,128)S(1)}, f32[64]{0:T(128)S(1)}) all-reduce(f32[64,64]{1,0:T(8,128)S(1)} %fusion.77, f32[64]{0:T(128)S(1)} %convolution_bitcast_fusion.3), channel_id=1, replica_groups=mesh['member'=16,'tile'=16] {'member','tile'}, use_global_device_ids=true, to_apply=%region_2.3 | all-reduce | flops 4160 | bytes 33280 | tf_op jit(solution)/shard_map/psum | solution.py:166
  427.7 0.6 fusion.92
  429.0 5.8 %cholesky.14 = f32[64,64]{1,0:T(8,128)S(1)} custom-call(f32[64,64]{1,0:T(8,128)S(1)} %get-tuple-element.65), custom_call_target="Cholesky" | custom-call | tf_op jit(solution)/shard_map/jit(cholesky)/cholesky | solution.py:53
  434.9 0.6 compare_reduce_fusion
  435.6 0.7 fusion.88
  436.2 4.9 %custom-call.10 = f32[1,64,64]{1,2,0:T(8,128)S(1)} custom-call(f32[1,64,64]{2,1,0:T(8,128)S(1)} %fusion.88), custom_call_target="InvertDiagBlocksLowerTriangular" | custom-call | tf_op jit(solution)/shard_map/jit(_cho_solve)/triangular_solve | solution.py:54
  441.5 15.5 %while.13 = (s32[]{:T(128)}, f32[64,64]{0,1:T(8,128)S(1)}, f32[64,64]{1,0:T(8,128)S(1)}, s32[]{:T(128)}) while((s32[]{:T(128)}, f32[64,64]{0,1:T(8,128)S(1)}, f32[64,64]{1,0:T(8,128)S(1)}, s32[]{:T(128)}) %tuple.32), condition=%wide.region_5.6_spmd.clone, body=%wide.region_4.5_spmd.clone.sunk | while | flops 9453570 | bytes 213045 | solution.py:65
  441.6 0.2 fusion.166
  441.9 0.2 convolution_bitcast_fusion.5
  442.2 0.2 fusion.166
  442.6 0.2 convolution_bitcast_fusion.5
  443.2 0.2 convolution_bitcast_fusion.5
  443.5 0.2 fusion.166
  443.9 0.2 convolution_bitcast_fusion.5
  444.5 0.2 convolution_bitcast_fusion.5
  444.8 0.2 fusion.166
  445.2 0.2 convolution_bitcast_fusion.5
  445.8 0.2 convolution_bitcast_fusion.5
  446.1 0.2 fusion.166
  446.4 0.2 convolution_bitcast_fusion.5
  447.1 0.2 convolution_bitcast_fusion.5
  447.7 0.2 convolution_bitcast_fusion.5
  448.4 0.2 convolution_bitcast_fusion.5
  449.0 0.2 convolution_bitcast_fusion.5
  449.7 0.2 convolution_bitcast_fusion.5
  450.3 0.2 convolution_bitcast_fusion.5
  451.0 0.2 convolution_bitcast_fusion.5
  451.6 0.2 convolution_bitcast_fusion.5
  452.2 0.2 convolution_bitcast_fusion.5
  452.9 0.2 convolution_bitcast_fusion.5
  453.5 0.2 convolution_bitcast_fusion.5
  454.2 0.2 convolution_bitcast_fusion.5
  454.8 0.2 convolution_bitcast_fusion.5
  455.5 0.2 convolution_bitcast_fusion.5
  456.1 0.2 convolution_bitcast_fusion.5
  456.8 0.2 convolution_bitcast_fusion.5
  457.0 0.9 convert_reduce_fusion
  458.0 7.6 %add_convert_fusion.1 = bf16[73,135,64]{0,2,1:T(8,128)(2,1)} fusion(bf16[73,135,64]{0,1,2:T(8,128)(2,1)} %bitcast.170, f32[73,135]{0,1:T(8,128)S(1)} %broadcast_multiply_fusion, f32[64,64]{1,0:T(8,128)S(1)} %get-tuple-element.27, f32[64]{0:T(128)S(1)} %fusion.51, f32[]{:T(128)S(6)} %sqrt.7), kind=kOutput, calls=%fused_computation.24 | convolution fusion | flops 486924032 | bytes 2578944 | tf_op jit(solution)/shard_map/ckf,fn->ckn/dot_general | solution.py:72
  (130 shorter events, 8.6 us)
Async XLA Ops:
  0.0 282.5 %copy-start = (bf16[512,256]{1,0:T(8,128)(2,1)S(1)}, bf16[512,256]{1,0:T(8,128)(2,1)}, u32[]{:S(2)}) copy-start(bf16[512,256]{1,0:T(8,128)(2,1)} %param.17) | copy-start | bytes 786436
  13.2 10.1 %copy-start.6 = (f32[256,96]{0,1:T(8,128)S(1)}, f32[256,96]{0,1:T(8,128)}, u32[]{:S(2)}) copy-start(f32[256,96]{0,1:T(8,128)} %param.15) | copy-start | bytes 294916
  13.2 115.0 %all-to-all-start = ((bf16[4,256,6,360]{3,0,2,1:T(4,128)(2,1)}), bf16[4,256,6,360]{3,0,2,1:T(4,128)(2,1)}, u32[]{:S(2)}, u32[]{:S(2)}) async-start(bf16[4,256,6,360]{3,0,2,1:T(4,128)(2,1)} %copy.128), calls=%async_computation | async-start | bytes 9437184 | tf_op jit(solution)/shard_map/all_to_all | solution.py:105
  273.1 9.4 %copy-start.8 = (bf16[256,512]{1,0:T(8,128)(2,1)S(1)}, bf16[256,512]{1,0:T(8,128)(2,1)}, u32[]{:S(2)}) copy-start(bf16[256,512]{1,0:T(8,128)(2,1)} %param.16) | copy-start | bytes 786436
  282.6 12.3 %copy-start.2 = (bf16[4,73,6,360]{3,0,2,1:T(4,128)(2,1)S(1)}, bf16[4,73,6,360]{3,0,2,1:T(4,128)(2,1)}, u32[]{:S(2)}) copy-start(bf16[4,73,6,360]{3,0,2,1:T(4,128)(2,1)} %param.13) | copy-start | bytes 3784324
  282.6 12.3 %copy-start.4 = (bf16[256,73]{0,1:T(8,128)(2,1)S(1)}, bf16[256,73]{0,1:T(8,128)(2,1)}, u32[]{:S(2)}) copy-start(bf16[256,73]{0,1:T(8,128)(2,1)} %param.18) | copy-start | bytes 112132
  303.9 10.1 %copy-start.5 = (f32[1,128,73]{1,0,2:T(1,128)S(1)}, f32[1,128,73]{1,0,2:T(1,128)}, u32[]{:S(2)}) copy-start(f32[1,128,73]{1,0,2:T(1,128)} %param.21) | copy-start | bytes 112132
  303.9 10.7 %copy-start.9 = (f32[1,128]{1,0:T(1,128)S(1)}, f32[1,128]{1,0:T(1,128)}, u32[]{:S(2)}) copy-start(f32[1,128]{1,0:T(1,128)} %param.23) | copy-start | bytes 1540
  307.2 42.1 %all-to-all-start.2 = ((bf16[73,16,135,4]{0,3,2,1:T(4,128)(2,1)}), bf16[73,16,135,4]{0,3,2,1:T(4,128)(2,1)S(1)}, u32[]{:S(2)}, u32[]{:S(2)}) async-start(bf16[73,16,135,4]{0,3,2,1:T(4,128)(2,1)} %bitcast.167), calls=%async_computation.2 | async-start | bytes 4423680 | tf_op jit(solution)/shard_map/all_to_all | solution.py:161
  313.9 38.8 %copy-start.10 = (s32[1,128]{1,0:T(1,128)S(1)}, s32[1,128]{1,0:T(1,128)}, u32[]{:S(2)}) copy-start(s32[1,128]{1,0:T(1,128)} %param.20) | copy-start | bytes 1540
  349.9 4.4 copy-start.7
  351.3 1.4 copy-start.3
  441.5 24.1 %copy-start.1 = (bf16[512,256]{1,0:T(8,128)(2,1)S(1)}, bf16[512,256]{1,0:T(8,128)(2,1)}, u32[]{:S(2)}) copy-start(bf16[512,256]{1,0:T(8,128)(2,1)} %param.17) | copy-start | bytes 786436
where the time goes:
time: 466 us
  blocking collectives  186 us (40%)
  waiting for transfers between devices  138 us (30%)
  matrix products  65.6 us (14%)
  local copies, waits for them, and re-layouts  40.4 us (9%)
  starting transfers between devices  16.9 us (4%)
  other arithmetic  16.3 us (3%)
    all_to_all x1, blocking collectives, shards(): lax.all_to_all(spatial_band, 'tile', split_axis=2, concat_axis=1, tiled=T...  112 us
    all_to_all x1, waiting for transfers between devices, shards(): lax.all_to_all(latent_features, 'tile', split_axis=1, concat_axis=2, tile...  103 us
    psum x1, blocking collectives, shards(): gram, innov = lax.psum((gram, innov), ('member', 'tile'))  73.1 us
    all_to_all x1, waiting for transfers between devices, shards(): lax.all_to_all(sorted_lines, 'member', split_axis=1, concat_axis=3, tiled...  34.6 us
    convert_element_type x2, local copies, waits for them, and re-layouts, shards(): physical_space_values.astype(predicted_values)  14.3 us
    dot_general x1, matrix products, shards(): jnp.einsum('auzo,uf->afzo', nested_body, second_layer_matrix, preferred_e...  12.2 us
    all_to_all x1, starting transfers between devices, shards(): lax.all_to_all(latent_features, 'tile', split_axis=1, concat_axis=2, tile...  10.1 us
  transfers between devices with their start and end apart: 2, of which 2 were waited for; matrix products, arithmetic and copies ran while one was open for 0% of the time, Pallas kernels for 0%

commit v1 on v0

v1 whole, which is shorter than its diff:
```python
import functools
import math

import jax
import jax.numpy as jnp
import numpy as np
from jax import lax
from jax.experimental import pallas as pl
from jax.experimental.pallas import tpu as pltpu
from jax.sharding import PartitionSpec as P

MMAX = 96
NS_ITERS = 24
BF = jnp.bfloat16
F32 = jnp.float32
HI = lax.Precision.HIGHEST
MESH = pl.DeviceIdType.MESH


def lon_tables(nlon, mmax):
    lon = np.arange(nlon, dtype=np.float64)
    wave = np.arange(mmax, dtype=np.float64)
    phase = np.mod(lon[:, None] * wave[None, :], float(nlon))
    angle = 2.0 * math.pi * phase / nlon
    forward = np.concatenate([np.cos(angle), -np.sin(angle)], axis=1)
    factor = np.where(wave == 0.0, 1.0, 2.0) / nlon
    inverse = np.concatenate([np.cos(angle) * factor, -np.sin(angle) * factor], axis=1).T
    return (forward.astype(np.float32).astype(BF), inverse.astype(np.float32).astype(BF))


def lat_tables(nlat):
    row = np.arange(nlat, dtype=np.float64)
    phase = np.mod((2.0 * row[:, None] + 1.0) * row[None, :], float(4 * nlat))
    basis = np.cos(math.pi * phase / (2.0 * nlat))
    factor = np.where(row == 0.0, 1.0, 2.0) / nlat
    forward = (basis * factor[None, :]).T
    return (forward.astype(np.float32).astype(BF), basis.astype(np.float32).astype(BF))


def reduce_kernel(nm, nt, part_ref, out_ref, got, mid, midg, fin, ssem, rsem):
    m, t = lax.axis_index("member"), lax.axis_index("tile")
    bar = pltpu.get_barrier_semaphore()

    def tile_peer(i):
        return (m, lax.rem(t + i, nt))

    def member_peer(i):
        return (lax.rem(m + i, nm), t)

    for i in range(1, nt):
        pl.semaphore_signal(bar, inc=1, device_id=tile_peer(i), device_id_type=MESH)
    for i in range(1, nm):
        pl.semaphore_signal(bar, inc=1, device_id=member_peer(i), device_id_type=MESH)
    pl.semaphore_wait(bar, nt + nm - 2)

    def send(src, dst, phase, i, dev):
        return pltpu.make_async_remote_copy(
            src_ref=src, dst_ref=dst, send_sem=ssem.at[phase, i], recv_sem=rsem.at[phase, i],
            device_id=dev, device_id_type=MESH)

    one = []
    for i in range(1, nt):
        c = send(part_ref.at[lax.rem(t + i, nt)], got.at[i], 0, i, tile_peer(i))
        c.start()
        one.append(c)
    acc = part_ref[t]
    for c in one:
        c.wait_recv()
    for i in range(1, nt):
        acc = acc + got[i]
    mid[...] = acc
    two = []
    for i in range(1, nm):
        c = send(mid, midg.at[lax.rem(m, nm)], 1, i, member_peer(i))
        c.start()
        two.append(c)
    midg[m] = acc
    for c in two:
        c.wait_recv()
    tot = midg[0]
    for i in range(1, nm):
        tot = tot + midg[i]
    out_ref[t] = tot
    fin[...] = tot
    three = []
    for i in range(1, nt):
        c = send(fin, out_ref.at[t], 2, i, tile_peer(i))
        c.start()
        three.append(c)
    for c in three:
        c.wait_recv()
    for c in one + two + three:
        c.wait_send()


def all_sum(part, nm, nt):
    vm = pl.BlockSpec(memory_space=pltpu.VMEM)
    return pl.pallas_call(
        functools.partial(reduce_kernel, nm, nt),
        out_shape=jax.ShapeDtypeStruct(part.shape, F32),
        in_specs=[vm],
        out_specs=vm,
        scratch_shapes=[
            pltpu.VMEM((nt, 8, 128), F32),
            pltpu.VMEM((8, 128), F32),
            pltpu.VMEM((nm, 8, 128), F32),
            pltpu.VMEM((8, 128), F32),
            pltpu.SemaphoreType.DMA((3, 16)),
            pltpu.SemaphoreType.DMA((3, 16)),
        ],
        compiler_params=pltpu.CompilerParams(collective_id=0, has_side_effects=True),
        name="all_sum",
    )(part)


def mix_of(stats, n):
    rows = lax.broadcasted_iota(jnp.int32, (n, n), 0)
    cols = lax.broadcasted_iota(jnp.int32, (n, n), 1)
    eye = (rows == cols).astype(F32)
    rw = lax.broadcasted_iota(jnp.int32, (n, 128), 0)
    cw = lax.broadcasted_iota(jnp.int32, (n, 128), 1)
    wide = jnp.where(cw < n, stats / (n - 1.0) + (rw == cw).astype(F32), stats)
    system = wide[:, :n]
    scale = jnp.sqrt(jnp.sum(system * system))
    up, root = system / scale, eye
    done = 0
    for it in range(NS_ITERS):
        shift = 1.5 * eye - 0.5 * jnp.dot(root, up, precision=HI, preferred_element_type=F32)
        up = jnp.dot(up, shift, precision=HI, preferred_element_type=F32)
        root = jnp.dot(shift, root, precision=HI, preferred_element_type=F32)
        upto = min(n, -(-n * (it + 1) // NS_ITERS))
        for j in range(done, upto):
            r = wide[j:j + 1, :]
            r = r / wide[j:j + 1, j:j + 1]
            col = wide[:, j:j + 1] - (rw[:, :1] == j).astype(F32)
            wide = wide - col * r
        done = upto
    weight = wide[:, n:n + 1] / (n - 1.0)
    return root / jnp.sqrt(scale) + weight


def mix_kernel(stats_ref, mix_ref):
    mix_ref[...] = mix_of(stats_ref[...], mix_ref.shape[0])


def mix_call(stats, n):
    vm = pl.BlockSpec(memory_space=pltpu.VMEM)
    return pl.pallas_call(
        mix_kernel,
        out_shape=jax.ShapeDtypeStruct((n, n), F32),
        in_specs=[vm],
        out_specs=vm,
        name="mix",
    )(stats)


def tile_terms(patch, count, cells, obs_op, value, error):
    ncell = patch.shape[1]
    sel = (cells[:, None] == jnp.arange(ncell, dtype=jnp.int32)[None, :]).astype(BF)
    picked = jnp.einsum("zv,rvg->zrg", sel, patch, preferred_element_type=F32)
    counterpart = jnp.einsum("jc,jcn->jn", obs_op, picked, precision=HI)
    center = jnp.mean(counterpart, axis=1)
    spread = counterpart - center[:, None]
    live = jnp.arange(obs_op.shape[0], dtype=jnp.int32) < count
    weight = jnp.where(live, 1.0 / error, jnp.zeros_like(error))
    both = jnp.concatenate([spread, (value - center)[:, None]], axis=1)
    return jnp.dot((spread * weight[:, None]).T, both, precision=HI)


def update(patch, mix):
    base = patch.astype(F32)
    center = jnp.mean(base, axis=2, keepdims=True)
    moved = jnp.einsum("ckf,fn->ckn", base - center, mix, precision=HI)
    return (center + moved).astype(BF)


def shards(x, lift, gain, w1, w2, readout, obs_count, obs_cell, obs_op, obs_value, obs_error):
    mem, nvar, rows, nlon = x.shape
    nt, nm = lax.axis_size("tile"), lax.axis_size("member")
    nlat = rows * nt
    emb = lift.shape[1]
    t = lax.axis_index("tile")
    lon_f, lon_i = (jnp.asarray(a) for a in lon_tables(nlon, MMAX))
    lat_f, lat_i = (jnp.asarray(a) for a in lat_tables(nlat))
    k = 2 * MMAX
    own = rows * nvar
    hatx = jnp.einsum("mcpq,qk->pcmk", x, lon_f, preferred_element_type=F32).astype(BF)
    hatx = jnp.pad(hatx.reshape(own, mem * k), ((0, 448 - own), (0, 0)))
    hats = lax.all_gather(hatx, "tile", axis=0, tiled=True)
    band = lax.dynamic_slice_in_dim(lat_i, t * rows, rows, 0).astype(F32)
    g = (band[:, None, :] * gain[None, :, :]).reshape(rows * emb, nlat)
    tr = jnp.dot(g, lat_f.astype(F32), precision=HI)
    w = tr.reshape(rows, emb, nt, rows, 1) * lift.T.astype(F32)[None, :, None, None, :]
    w = w.astype(BF).reshape(rows * emb, nt, own)
    w = jnp.pad(w, ((0, 0), (0, 0), (0, 448 - own))).reshape(rows * emb, nt * 448)
    back = jnp.dot(w, hats, preferred_element_type=F32).astype(BF).reshape(rows, emb, mem, k)
    spatial = jnp.einsum("pemk,kq->mepq", back, lon_i, preferred_element_type=F32).astype(BF)
    hid = jnp.einsum("mcpq,ce->mepq", x, lift, preferred_element_type=F32).astype(BF)
    mixed = (hid.astype(F32) + spatial.astype(F32)).astype(BF)
    inner = jax.nn.gelu(jnp.einsum("mepq,eh->mhpq", mixed, w1, preferred_element_type=F32)).astype(BF)
    outer = (mixed.astype(F32) + jnp.einsum("mhpq,he->mepq", inner, w2, preferred_element_type=F32)).astype(BF)
    lifted = jnp.einsum("mepq,ec->cpqm", outer, readout, preferred_element_type=F32)
    forecast = (jnp.transpose(x, (1, 2, 3, 0)).astype(F32) + lifted).astype(BF)
    ncell = rows * nlon // nm
    lines = forecast.reshape(nvar, nm, ncell, mem)
    patch = lax.all_to_all(lines, "member", split_axis=1, concat_axis=3, tiled=True)
    patch = patch.reshape(nvar, ncell, mem * nm)
    n = mem * nm
    part = tile_terms(patch, obs_count[0], obs_cell[0], obs_op[0], obs_value[0], obs_error[0])
    part = jnp.pad(part.reshape(nt, n // nt, n + 1), ((0, 0), (0, 8 - n // nt), (0, 127 - n)))
    stats = all_sum(part, nm, nt)[:, : n // nt].reshape(n, 128)
    return update(patch, mix_call(stats, n))


def solution(mesh):
    placed = (
        P("member", None, "tile", None),
        P(), P(), P(), P(), P(),
        P(("tile", "member")),
        P(("tile", "member"), None),
        P(("tile", "member"), None, None),
        P(("tile", "member"), None),
        P(("tile", "member"), None),
    )
    return jax.shard_map(
        shards, mesh=mesh, in_specs=placed, out_specs=P(None, ("tile", "member"), None), check_vma=False)
```

time: 466 us -> 291 us (0.62)
  blocking collectives: 186 us -> 0 us
  waiting for transfers between devices: 138 us -> 31.5 us
  local copies, waits for them, and re-layouts: 40.4 us -> 118 us
  Pallas kernels: 0 us -> 35.4 us
  between operations: 1.64 us -> 14.3 us
  starting transfers between devices: 16.9 us -> 7.89 us
  other arithmetic: 16.3 us -> 23.4 us
  matrix products: 65.6 us -> 58.9 us
    all_to_all x1 -> x0, blocking collectives: 112 us -> none  [shards(): lax.all_to_all(spatial_band, 'tile', split_axis=2, concat_axis=1, tiled=T...]
    all_to_all x2 -> x1, waiting for transfers between devices: 138 us -> 31.4 us  [shards(): lax.all_to_all(lines, 'member', split_axis=1, concat_axis=3, tiled=True)]
    mul x0 -> x3, local copies, waits for them, and re-layouts: none -> 73.6 us  [shards(): tr.reshape(rows, emb, nt, rows, 1)]
    psum x1 -> x0, blocking collectives: 73.1 us -> none  [shards(): gram, innov = lax.psum((gram, innov), ('member', 'tile'))]
    pallas_call x0 -> x2, Pallas kernels: none -> 35.4 us  [the longest x1 25.2 us: all_sum(): pl.pallas_call(functools.partial(reduce_kernel, nm, nt), out_shape=jax.Sh...]
    convert_element_type x4 -> x1, local copies, waits for them, and re-layouts: 26.7 us -> 0.7 us  [shards(): jnp.einsum('mcpq,qk->pcmk', x, lon_f, preferred_element_type=F32).astype(BF)]
    convert_element_type x2 -> x3, other arithmetic: 1.28 us -> 22.4 us  [the longest x1 21.7 us: shards(): w = w.astype(BF).reshape(rows * emb, nt, own)]
    unnamed x24 -> x30, local copies, waits for them, and re-layouts: 1.54 us -> 18.2 us
  transfers between devices with their start and end apart: 2 -> 2, of which waited for: 2 -> 1; matrix products, arithmetic and copies ran while one was open for 0% -> 43% of each run, Pallas kernels for 0% -> 0%
where the time goes in v1:
time: 291 us; the launch traced here: 289 us
  local copies, waits for them, and re-layouts  118 us (41%)
  matrix products  58.9 us (20%)
  Pallas kernels  35.4 us (12%)
  waiting for transfers between devices  31.5 us (11%)
  other arithmetic  23.4 us (8%)
  between operations  14.3 us (5%)
  starting transfers between devices  7.89 us (3%)
    mul x3, local copies, waits for them, and re-layouts, shards(): tr.reshape(rows, emb, nt, rows, 1)  73.6 us
    all_to_all x1, waiting for transfers between devices, shards(): lax.all_to_all(lines, 'member', split_axis=1, concat_axis=3, tiled=True)  31.4 us
    pallas_call x1, Pallas kernels, all_sum(): pl.pallas_call(functools.partial(reduce_kernel, nm, nt), out_shape=jax.Sh...  25.2 us
    dot_general x1, matrix products, shards(): jnp.dot(w, hats, preferred_element_type=F32).astype(BF)  24.5 us
    convert_element_type x1, other arithmetic, shards(): w = w.astype(BF).reshape(rows * emb, nt, own)  21.7 us
    unnamed x30, local copies, waits for them, and re-layouts  18.2 us
    dot_general x1, matrix products, shards(): jnp.einsum('mhpq,he->mepq', inner, w2, preferred_element_type=F32)  10.3 us
    pallas_call x1, Pallas kernels, mix_call(): pl.pallas_call(mix_kernel, out_shape=jax.ShapeDtypeStruct((n, n), F32), i...  10.1 us
  transfers between devices with their start and end apart: 2, of which 1 were waited for; matrix products, arithmetic and copies ran while one was open for 43% of the time, Pallas kernels for 0%

profile of v1, /device:TPU:1, one launch (start us, length us, event | category | flops | bytes accessed | tf_op | source)
XLA Modules:
  0.0 289.2 jit_solution(12224427758739975987)
XLA Ops:
  6.5 0.0 copy-start
  6.5 0.0 copy-start.8
  6.5 0.0 copy-start.5
  6.5 0.0 all-gather.2.cloned.1.call-start
  6.5 2.2 fusion.28
  8.7 0.7 copy.96
  9.4 1.0 reshape.80
  10.4 0.9 pad.13
  11.3 0.0 all-gather.2.cloned.1.call-update
  11.3 0.7 dynamic-slice_convert_fusion
  12.0 0.0 copy-done.8
  12.0 0.0 copy-done.5
  12.0 0.5 fusion.31
  12.6 0.4 copy.93
  12.9 18.7 %mul.71 = f32[6,256,16,6,73]{1,0,2,4,3:T(8,128)} broadcast(f32[6,256,16,6]{1,0,2,3:T(8,128)S(1)} %copy.93), dimensions={0,1,2,3} | broadcast | bytes 43646976 | tf_op jit(solution)/shard_map/mul | solution.py:193
  31.6 0.0 copy-start.4
  31.6 54.6 %mul.72 = f32[1536,16,438]{0,1,2:T(8,128)} reshape(f32[6,256,16,6,73]{1,0,2,4,3:T(8,128)} %mul.71) | data formatting | bytes 86114304 | tf_op jit(solution)/shard_map/mul | solution.py:193
  86.2 0.0 copy-done.4
  86.3 0.2 mul.73
  86.5 0.2 pad.17
  86.7 1.2 copy.132
  88.0 21.7 %multiply_convert_fusion = bf16[1536,16,438]{0,1,2:T(8,128)(2,1)} fusion(f32[1536,16,438]{0,1,2:T(8,128)} %mul.72, f32[1536,438]{0,1:T(8,128)S(1)} %bitcast.106), kind=kLoop, calls=%fused_computation | loop fusion | flops 21528576 | bytes 67276800 | tf_op jit(solution)/shard_map/convert_element_type | solution.py:194
  109.7 15.3 %copy.130 = bf16[1536,16,438]{0,2,1:T(8,128)(2,1)S(1)} copy(bf16[1536,16,438]{0,1,2:T(8,128)(2,1)} %multiply_convert_fusion) | data formatting | bytes 43057152
  125.0 9.4 %pad.12.clone = bf16[1536,16,448]{0,2,1:T(8,128)(2,1)} pad(bf16[1536,16,438]{0,2,1:T(8,128)(2,1)S(1)} %copy.130, bf16[]{:T(256)} %constant.10.clone.1), padding=0_0x0_0x0_10 | pad | bytes 43548672 | tf_op jit(solution)/shard_map/jit(_pad)/pad | solution.py:195
  134.4 0.0 all-gather.2.cloned.1.call-done
  134.4 24.5 %convolution_convert_fusion = bf16[1536,768]{1,0:T(8,128)(2,1)} fusion(bf16[1536,7168]{0,1:T(8,128)(2,1)} %bitcast.103, bf16[7168,768]{1,0:T(8,128)(2,1)} %all-gather.2.cloned.1.call-done), kind=kOutput, calls=%fused_computation.22 | convolution fusion | flops 16912613376 | bytes 35389440 | tf_op jit(solution)/shard_map/dot_general | solution.py:196
  159.0 6.3 %reshape.98 = bf16[6,256,4,192]{3,2,1,0:T(4,128)(2,1)S(1)} reshape(bf16[1536,768]{1,0:T(8,128)(2,1)} %convolution_convert_fusion) | data formatting | bytes 4718592 | tf_op jit(solution)/shard_map/reshape | solution.py:196
  165.3 0.0 copy-start.1
  165.3 2.4 fusion.19
  167.7 0.0 copy-done.1
  167.7 0.0 copy-start.9
  167.7 3.5 %fusion.9 = bf16[4,256,6,360]{1,3,2,0:T(8,128)(2,1)} fusion(bf16[6,256,4,360]{1,3,0,2:T(8,128)(2,1)S(1)} %fusion.19, bf16[4,73,6,360]{3,0,2,1:T(4,128)(2,1)S(1)} %copy-done.1, bf16[73,256]{1,0:T(8,128)(2,1)S(1)} %copy-done.4), kind=kOutput, calls=%fused_computation.13 | convolution fusion | flops 333987840 | bytes 10146176 | tf_op jit(solution)/shard_map/mcpq,ce->mepq/dot_general | solution.py:198
  171.2 0.0 copy-done
  171.2 0.0 copy-done.9
  171.2 0.0 copy-start.2
  171.2 0.0 copy-start.6
  171.2 10.3 %fusion.10 = f32[4,6,360,256]{3,2,1,0:T(8,128)} fusion(bf16[4,256,6,360]{1,3,2,0:T(8,128)(2,1)} %fusion.9, bf16[512,256]{1,0:T(8,128)(2,1)S(1)} %copy-done, bf16[256,512]{1,0:T(8,128)(2,1)S(1)} %copy-done.9), kind=kOutput, calls=%fused_computation.14 | convolution fusion | flops 4569661440 | bytes 13795328 | tf_op jit(solution)/shard_map/mhpq,he->mepq/dot_general | solution.py:201
  181.5 0.0 copy-done.2
  181.5 0.0 copy-done.6
  181.5 6.4 %fusion.21 = bf16[73,6,360,4]{2,0,1,3:T(8,128)(2,1)S(1)} fusion(f32[4,6,360,256]{3,2,1,0:T(8,128)} %fusion.10, bf16[4,256,6,360]{1,3,2,0:T(8,128)(2,1)} %fusion.9, bf16[4,73,6,360]{3,0,2,1:T(4,128)(2,1)S(1)} %copy-done.2, bf16[256,73]{0,1:T(8,128)(2,1)S(1)} %copy-done.6), kind=kOutput, calls=%fused_computation.26 | convolution fusion | flops 331456320 | bytes 15831296 | tf_op jit(solution)/shard_map/mepq,ec->cpqm/dot_general | solution.py:202
  187.8 0.0 copy-start.7
  187.9 0.0 copy-start.10
  187.9 3.3 %copy.124 = bf16[73,6,360,4]{0,3,2,1:T(4,128)(2,1)} copy(bf16[73,6,360,4]{2,0,1,3:T(8,128)(2,1)S(1)} %fusion.21) | data formatting | bytes 2522880 | tf_op jit(solution)/shard_map/reshape | solution.py:205
  191.1 7.9 %all-to-all-start = ((bf16[73,16,135,4]{0,3,2,1:T(4,128)(2,1)}), bf16[73,16,135,4]{0,3,2,1:T(4,128)(2,1)S(1)}, u32[]{:S(2)}, u32[]{:S(2)}) async-start(bf16[73,16,135,4]{0,3,2,1:T(4,128)(2,1)} %bitcast.107), calls=%async_computation | async-start | bytes 4423680 | tf_op jit(solution)/shard_map/all_to_all | solution.py:206
  199.0 0.0 copy-done.7
  199.7 0.0 copy-done.10
  199.7 0.0 copy-start.11
  199.7 31.4 %all-to-all-done = bf16[73,16,135,4]{0,3,2,1:T(4,128)(2,1)S(1)} async-done(((bf16[73,16,135,4]{0,3,2,1:T(4,128)(2,1)}), bf16[73,16,135,4]{0,3,2,1:T(4,128)(2,1)S(1)}, u32[]{:S(2)}, u32[]{:S(2)}) %all-to-all-start) | async-done | bytes 1261472 | tf_op jit(solution)/shard_map/all_to_all | solution.py:206
  231.2 0.7 copy.148
  231.8 0.0 copy-start.12
  231.8 1.4 copy.105
  233.3 0.0 copy-start.3
  233.3 1.4 copy-done.3
  234.7 0.0 copy-done.11
  234.7 1.4 multiply_reduce_fusion
  236.1 0.0 copy-done.12
  236.1 0.2 fusion.43
  236.3 0.6 pad.14.part_ref
  236.9 25.2 %all_sum.1 = f32[16,8,128]{2,1,0:T(8,128)} custom-call(f32[16,8,128]{2,1,0:T(8,128)} %pad.14.part_ref), custom_call_target="tpu_custom_call" | custom-call | tf_op jit(solution)/shard_map/all_sum/pallas_call | solution.py:98
  262.2 1.5 slice.3
  263.6 10.1 %mix.1 = f32[64,64]{1,0:T(8,128)} custom-call(f32[64,128]{1,0:T(8,128)} %bitcast.112), custom_call_target="tpu_custom_call" | custom-call | tf_op jit(solution)/shard_map/mix/pallas_call | solution.py:148
  273.8 0.9 convert_reduce_fusion
  274.7 7.6 %add_convert_fusion = bf16[73,135,64]{0,2,1:T(8,128)(2,1)} fusion(bf16[73,135,64]{0,1,2:T(8,128)(2,1)} %bitcast.110, f32[73,135]{0,1:T(8,128)S(1)} %broadcast_multiply_fusion, f32[64,64]{1,0:T(8,128)} %mix.1), kind=kOutput, calls=%fused_computation.17 | convolution fusion | flops 486915840 | bytes 2578684 | tf_op jit(solution)/shard_map/ckf,fn->ckn/dot_general | solution.py:173
  (8 shorter events, 0.1 us)
Async XLA Ops:
  6.5 164.7 %copy-start = (bf16[512,256]{1,0:T(8,128)(2,1)S(1)}, bf16[512,256]{1,0:T(8,128)(2,1)}, u32[]{:S(2)}) copy-start(bf16[512,256]{1,0:T(8,128)(2,1)} %param.19) | copy-start | bytes 786436
  6.5 5.5 %copy-start.8 = (bf16[16,6,96,1]{2,0,1,3:T(8,128)(2,1)S(1)}, bf16[16,6,96,1]{2,0,1,3:T(8,128)(2,1)}, u32[]{:S(2)}) copy-start(bf16[16,6,96,1]{2,0,1,3:T(8,128)(2,1)} %constant.57) | copy-start | bytes 55300
  6.5 5.5 %copy-start.5 = (f32[256,96]{0,1:T(8,128)S(1)}, f32[256,96]{0,1:T(8,128)}, u32[]{:S(2)}) copy-start(f32[256,96]{0,1:T(8,128)} %param.17) | copy-start | bytes 294916
  6.5 127.9 %all-gather.2.cloned.1.call-start = ((), (), s32[]{:S(2)}) async-start(), calls=%async_computation.1 | async-start | bytes 11698176 | tf_op jit(solution)/shard_map/all_gather | solution.py:189
  31.6 54.6 %copy-start.4 = (bf16[73,256]{1,0:T(8,128)(2,1)S(1)}, bf16[73,256]{1,0:T(8,128)(2,1)}, u32[]{:S(2)}) copy-start(bf16[73,256]{1,0:T(8,128)(2,1)} %param.16) | copy-start | bytes 112132
  165.3 2.4 copy-start.1
  167.7 3.5 %copy-start.9 = (bf16[256,512]{1,0:T(8,128)(2,1)S(1)}, bf16[256,512]{1,0:T(8,128)(2,1)}, u32[]{:S(2)}) copy-start(bf16[256,512]{1,0:T(8,128)(2,1)} %param.18) | copy-start | bytes 786436
  171.2 10.3 %copy-start.2 = (bf16[4,73,6,360]{3,0,2,1:T(4,128)(2,1)S(1)}, bf16[4,73,6,360]{3,0,2,1:T(4,128)(2,1)}, u32[]{:S(2)}) copy-start(bf16[4,73,6,360]{3,0,2,1:T(4,128)(2,1)} %param.15) | copy-start | bytes 3784324
  171.2 10.3 %copy-start.6 = (bf16[256,73]{0,1:T(8,128)(2,1)S(1)}, bf16[256,73]{0,1:T(8,128)(2,1)}, u32[]{:S(2)}) copy-start(bf16[256,73]{0,1:T(8,128)(2,1)} %param.20) | copy-start | bytes 112132
  187.8 11.2 %copy-start.7 = (f32[1,128,73]{1,0,2:T(1,128)S(1)}, f32[1,128,73]{1,0,2:T(1,128)}, u32[]{:S(2)}) copy-start(f32[1,128,73]{1,0,2:T(1,128)} %param.23) | copy-start | bytes 112132
  187.9 11.8 %copy-start.10 = (f32[1,128]{1,0:T(1,128)S(1)}, f32[1,128]{1,0:T(1,128)}, u32[]{:S(2)}) copy-start(f32[1,128]{1,0:T(1,128)} %param.25) | copy-start | bytes 1540
  191.1 40.0 %all-to-all-start = ((bf16[73,16,135,4]{0,3,2,1:T(4,128)(2,1)}), bf16[73,16,135,4]{0,3,2,1:T(4,128)(2,1)S(1)}, u32[]{:S(2)}, u32[]{:S(2)}) async-start(bf16[73,16,135,4]{0,3,2,1:T(4,128)(2,1)} %bitcast.107), calls=%async_computation | async-start | bytes 4423680 | tf_op jit(solution)/shard_map/all_to_all | solution.py:206
  199.7 34.9 %copy-start.11 = (s32[1,128]{1,0:T(1,128)S(1)}, s32[1,128]{1,0:T(1,128)}, u32[]{:S(2)}) copy-start(s32[1,128]{1,0:T(1,128)} %param.22) | copy-start | bytes 1540
  231.8 4.2 %copy-start.12 = (f32[1,128]{1,0:T(1,128)S(1)}, f32[1,128]{1,0:T(1,128)}, u32[]{:S(2)}) copy-start(f32[1,128]{1,0:T(1,128)} %param.24) | copy-start | bytes 1540
  233.3 1.4 copy-start.3
Sparse Core Ops, SparseCore 0:
  11.4 72.4 all-gather.1

commit v2 on v1

v2 whole, which is shorter than its diff:
```python
import functools
import math

import jax
import jax.numpy as jnp
import numpy as np
from jax import lax
from jax.experimental import pallas as pl
from jax.experimental.pallas import tpu as pltpu
from jax.sharding import PartitionSpec as P

MMAX = 96
NS_ITERS = 24
BF = jnp.bfloat16
F32 = jnp.float32
HI = lax.Precision.HIGHEST
MESH = pl.DeviceIdType.MESH


def lon_tables(nlon, mmax):
    lon = np.arange(nlon, dtype=np.float64)
    wave = np.arange(mmax, dtype=np.float64)
    phase = np.mod(lon[:, None] * wave[None, :], float(nlon))
    angle = 2.0 * math.pi * phase / nlon
    forward = np.concatenate([np.cos(angle), -np.sin(angle)], axis=1)
    factor = np.where(wave == 0.0, 1.0, 2.0) / nlon
    inverse = np.concatenate([np.cos(angle) * factor, -np.sin(angle) * factor], axis=1).T
    return (forward.astype(np.float32).astype(BF), inverse.astype(np.float32).astype(BF))


def lat_tables(nlat):
    row = np.arange(nlat, dtype=np.float64)
    phase = np.mod((2.0 * row[:, None] + 1.0) * row[None, :], float(4 * nlat))
    basis = np.cos(math.pi * phase / (2.0 * nlat))
    factor = np.where(row == 0.0, 1.0, 2.0) / nlat
    forward = (basis * factor[None, :]).T
    return (forward.astype(np.float32).astype(BF), basis.astype(np.float32).astype(BF))


VARS, CPAD = 73, 80
ROWS, NLON, NLAT = 6, 360, 96
KCOL = 2 * MMAX
CHUNK = 448
CELLS = 2304
EMB, HID = 256, 512
NZ = 8


def chunk_index():
    lat = np.full(CHUNK, -1)
    chan = np.full(CHUNK, -1)
    for p in range(ROWS):
        lat[64 * p:64 * p + 64], chan[64 * p:64 * p + 64] = p, np.arange(64)
        at = 384 + 9 * p
        lat[at:at + 9], chan[at:at + 9] = p, np.arange(64, 73)
    return lat, chan


def window(p):
    start = 128 * (360 * p // 128)
    return start, min(512, CELLS - start)


def kernel_tables():
    lon_f, lon_i = (np.asarray(a).astype(np.float32) for a in lon_tables(NLON, MMAX))
    lat_f, lat_i = (np.asarray(a).astype(np.float32) for a in lat_tables(NLAT))
    fw = np.zeros((ROWS, 512, 256), np.float32)
    for p in range(ROWS):
        at = 360 * p - window(p)[0]
        fw[p, at:at + 360, :KCOL] = lon_f
    iv = np.zeros((9, 2, 256, 256), np.float32)
    for n in range(9):
        low = min(256 * n // 360, 4)
        for s in range(2):
            for col in range(256):
                q = 256 * n + col - 360 * (low + s)
                if 0 <= q < 360:
                    iv[n, s, :KCOL, col] = lon_i[:, q]
    lat, chan = chunk_index()
    lf = np.zeros((16, 256, CHUNK), np.float32)
    for t in range(16):
        cols = lat_f[:, 6 * t + np.maximum(lat, 0)] * (lat >= 0)
        lf[t, :NLAT], lf[t, 128:128 + NLAT] = cols, cols
    lf = lf.reshape(NZ, 2, 256, CHUNK).transpose(0, 2, 1, 3).reshape(NZ, 256, 2 * CHUNK)
    li = np.zeros((NLAT, 128), np.float32)
    li[:, :NLAT] = lat_i
    return fw.astype(BF), iv.reshape(9, 512, 256).astype(BF), lf.astype(BF), li


def dot(a, b):
    return jnp.dot(a, b, preferred_element_type=F32)


def forecast_kernel(nm, x_ref, fw_ref, iv_ref, lf_ref, li_ref, gain_ref, lx_ref, lt_ref, w1_ref, w2_ref, ro_ref,
                    count_ref, cell_ref, op_ref, val_ref, err_ref,
                    field_ref, stats_ref,
                    spec, wmat, acc, bk, fs, cp, lx2, part, got, mid, midg, fin,
                    ag_s, ag_r, ax_s, ax_r, rs_s, rs_r):
    m, t = lax.axis_index("member"), lax.axis_index("tile")
    nt = 2 * NZ
    z, core = t // 2, lax.rem(t, 2)

    def zat(d):
        return lax.rem(z + d + NZ, NZ)

    def member_peer(i):
        return (lax.rem(m + i, nm), t)

    def tile_peer(i):
        return (m, lax.rem(t + i, nt))

    right, left, sib = (m, zat(1) * 2 + core), (m, zat(-1) * 2 + core), (m, z * 2 + 1 - core)
    bar = pltpu.get_barrier_semaphore()
    for i in range(1, nt):
        pl.semaphore_signal(bar, inc=1, device_id=tile_peer(i), device_id_type=MESH)
    for i in range(1, nm):
        pl.semaphore_signal(bar, inc=1, device_id=member_peer(i), device_id_type=MESH)

    low64 = lax.broadcasted_iota(jnp.int32, (CPAD, 128), 1) < 64

    def spectra(q):
        tails = []
        for p in range(ROWS):
            at, wide = window(p)
            v0 = dot(x_ref[2 * q, :, at:at + wide], fw_ref[p, :wide])
            v1 = dot(x_ref[2 * q + 1, :, at:at + wide], fw_ref[p, :wide])
            mixed = jnp.where(low64, v0[:, 128:], pltpu.roll(v1[:, 128:], 64, 1))
            v = jnp.concatenate([v0[:, :128], mixed, v1[:, :128]], axis=1)
            spec[q, t, 64 * p:64 * p + 64] = v[:64].astype(BF)
            tails.append(v[64:VARS])
        tails.append(jnp.zeros((10, 384), F32))
        spec[q, t, 384:CHUNK] = jnp.concatenate(tails, axis=0).astype(BF)

    sent = []

    def half(h):
        return pl.ds(0, CHUNK) if h is None else pl.ds(h * (CHUNK // 2), CHUNK // 2)

    def copy(q, dz, other, h, sem, dev):
        ref = spec.at[q, zat(dz) * 2 + (1 - core if other else core), half(h)]
        return pltpu.make_async_remote_copy(
            src_ref=ref, dst_ref=ref, send_sem=ag_s.at[q, sem], recv_sem=ag_r.at[q, sem],
            device_id=dev, device_id_type=MESH)

    def go(c):
        c.start()
        sent.append(c)

    def own(q):
        for h in range(2):
            go(copy(q, 0, False, h, h, right))
            go(copy(q, 0, False, h, 7 + h, left))
        go(copy(q, 0, False, None, 14, sib))

    def step(q, d, h):
        if d < 4 or h == 0:
            copy(q, -d, False, h, 2 * (d - 1) + h, right).wait_recv()
            if d < 3 or (d == 3 and h == 0):
                go(copy(q, -d, False, h, 2 * d + h, right))
        if d < 4 or h == 1:
            copy(q, d, False, h, 7 + (2 * (d - 1) + h if d < 4 else 6), left).wait_recv()
            if d < 3 or (d == 3 and h == 1):
                go(copy(q, d, False, h, 7 + (2 * d + h if d < 3 else 6), left))
        if d == 4:
            go(copy(q, 4, False, h, 21 + h, sib))
        elif h == 1:
            go(copy(q, -d, False, None, 14 + d, sib))
            go(copy(q, d, False, None, 17 + d, sib))

    def from_sib(q, d):
        if d == 0:
            copy(q, 0, True, None, 14, sib).wait_recv()
        elif d == 4:
            copy(q, 4, True, 0, 21, sib).wait_recv()
            copy(q, 4, True, 1, 22, sib).wait_recv()
        elif d < 0:
            copy(q, d, True, None, 14 - d, sib).wait_recv()
        else:
            copy(q, d, True, None, 17 + d, sib).wait_recv()

    def weights(d):
        zz = zat(d)

        @pl.loop(0, ROWS)
        def _(p):
            g = gain_ref[...] * li_ref[pl.ds(ROWS * t + p, 1), :]
            hi = g.astype(BF)
            lo = (g - hi.astype(F32)).astype(BF)
            w = dot(jnp.concatenate([hi, lo], axis=1), lf_ref[zz])
            wmat[zz, pl.ds(pl.multiple_of(p * EMB, EMB), EMB), :] = (w * lx2[...]).astype(BF)

    def apply(q, d):
        zz = zat(d)
        g = spec[q, pl.ds(zz * 2, 2)].reshape(2 * CHUNK, 384)

        @pl.loop(0, 3)
        def _(b):
            rows = pl.ds(pl.multiple_of(b * 512, 512), 512)
            v = dot(wmat[zz, rows, :], g)
            acc[q, rows, :] = v if d == 0 else acc[q, rows, :] + v

    c0 = math.sqrt(2.0 / math.pi)

    def member(e):
        q = e // 2

        @pl.loop(0, ROWS)
        def _(p):
            a = acc[q, pl.ds(pl.multiple_of(p * EMB, EMB), EMB), :]
            if e % 2:
                a = jnp.concatenate([a[:, 256:], pltpu.roll(a[:, 128:256], 64, 1)], axis=1)
            else:
                a = a[:, :256]
            bk[p] = a.astype(BF)

        @pl.loop(0, 9)
        def _(n):
            low = jnp.minimum(256 * n // 360, 4)
            lanes = pl.ds(pl.multiple_of(n * 256, 256), 256)
            x = x_ref[e, :, lanes]
            s = dot(jnp.concatenate([bk[low], bk[low + 1]], axis=1), iv_ref[n])
            mixed = (s + dot(lt_ref[...], x)).astype(BF)
            u = dot(w1_ref[...], mixed)
            u = 0.5 * u * (1.0 + jnp.tanh(c0 * (u + 0.044715 * (u * u * u))))
            outer = (mixed.astype(F32) + dot(w2_ref[...], u.astype(BF))).astype(BF)
            fs[e, :, lanes] = (x.astype(F32) + dot(ro_ref[...], outer)).astype(BF)

        for i in range(1, nm):
            go(out_copy(e, i))
        field_ref[4 * m + e] = fs[e, :, pl.ds(pl.multiple_of(128 * m, 128), 256)]

    def out_copy(e, i):
        to = lax.rem(m + i, nm)
        return pltpu.make_async_remote_copy(
            src_ref=fs.at[e, :, pl.ds(pl.multiple_of(128 * to, 128), 256)], dst_ref=field_ref.at[4 * m + e],
            send_sem=ax_s.at[e, i], recv_sem=ax_r.at[e, i], device_id=(to, t), device_id_type=MESH)

    spectra(0)
    pl.semaphore_wait(bar, nt + nm - 2)
    own(0)
    spectra(1)
    lx2[...] = lx_ref[...].astype(F32)
    for d in (0, 1, -1):
        weights(d)
    step(0, 1, 0)
    weights(2)
    step(0, 1, 1)
    weights(-2)
    from_sib(0, 0)
    apply(0, 0)
    step(0, 2, 0)
    weights(3)
    from_sib(0, 1)
    apply(0, 1)
    step(0, 2, 1)
    weights(-3)
    from_sib(0, -1)
    apply(0, -1)
    own(1)
    step(0, 3, 0)
    weights(4)
    from_sib(0, 2)
    apply(0, 2)
    step(0, 3, 1)
    from_sib(0, -2)
    apply(0, -2)
    step(0, 4, 0)
    step(0, 4, 1)
    from_sib(1, 0)
    apply(1, 0)
    from_sib(0, 3)
    apply(0, 3)
    step(1, 1, 0)
    from_sib(0, -3)
    apply(0, -3)
    step(1, 1, 1)
    from_sib(0, 4)
    apply(0, 4)
    step(1, 2, 0)
    member(0)
    step(1, 2, 1)
    from_sib(1, 1)
    apply(1, 1)
    from_sib(1, -1)
    apply(1, -1)
    step(1, 3, 0)
    member(1)
    step(1, 3, 1)
    from_sib(1, 2)
    apply(1, 2)
    from_sib(1, -2)
    apply(1, -2)
    step(1, 4, 0)
    step(1, 4, 1)
    from_sib(1, 3)
    apply(1, 3)
    from_sib(1, -3)
    apply(1, -3)
    from_sib(1, 4)
    apply(1, 4)
    member(2)
    member(3)

    cells = cell_ref[...] + 7 * m
    pick = (lax.broadcasted_iota(jnp.int32, (256, 128), 0) == cells).astype(BF)
    ident = (lax.broadcasted_iota(jnp.int32, (CPAD, VARS), 0)
             == lax.broadcasted_iota(jnp.int32, (CPAD, VARS), 1)).astype(F32)
    nt_dims = (((1,), (1,)), ((), ()))
    op = lax.dot_general(ident, op_ref[...], nt_dims, precision=HI, preferred_element_type=F32)

    def counterparts(e, src):
        f = 4 * src + e
        v = dot(field_ref[f], pick) * op
        cp[pl.ds(f, 1), :] = jnp.sum(v, axis=0, keepdims=True)

    for e in range(4):
        for i in range(nm):
            if i:
                out_copy(e, i).wait_recv()
            counterparts(e, lax.rem(m - i + nm, nm))
    c = cp[...]
    n = c.shape[0]
    ybar = jnp.mean(c, axis=0, keepdims=True)
    spread = c - ybar
    live = lax.broadcasted_iota(jnp.int32, (1, 128), 1) < count_ref[...]
    weight = jnp.where(live, 1.0 / err_ref[...], 0.0)
    both = jnp.concatenate([spread, val_ref[...] - ybar, jnp.zeros((127 - n, 128), F32)], axis=0)
    gram = lax.dot_general(spread * weight, both, nt_dims, precision=HI, preferred_element_type=F32)
    per = n // nt
    for b in range(nt):
        part[b, :per] = gram[per * b:per * b + per]
        part[b, per:] = jnp.zeros((8 - per, 128), F32)

    def send(src, dst, phase, i, dev):
        cc = pltpu.make_async_remote_copy(
            src_ref=src, dst_ref=dst, send_sem=rs_s.at[phase, i], recv_sem=rs_r.at[phase, i],
            device_id=dev, device_id_type=MESH)
        go(cc)
        return cc

    one = [send(part.at[lax.rem(t + i, nt)], got.at[i], 0, i, tile_peer(i)) for i in range(1, nt)]
    tot = part[t]
    for cc in one:
        cc.wait_recv()
    for i in range(1, nt):
        tot = tot + got[i]
    mid[...] = tot
    two = [send(mid, midg.at[m], 1, i, member_peer(i)) for i in range(1, nm)]
    midg[m] = tot
    for cc in two:
        cc.wait_recv()
    tot = midg[0]
    for i in range(1, nm):
        tot = tot + midg[i]
    stats_ref[t] = tot
    fin[...] = tot
    three = [send(fin, stats_ref.at[t], 2, i, tile_peer(i)) for i in range(1, nt)]
    for cc in three:
        cc.wait_recv()
    for cc in sent:
        cc.wait_send()


def forecast_call(args, nm, nt, n):
    vm = pl.BlockSpec(memory_space=pltpu.VMEM)
    dma = pltpu.SemaphoreType.DMA
    return pl.pallas_call(
        functools.partial(forecast_kernel, nm),
        out_shape=[jax.ShapeDtypeStruct((n, CPAD, 256), BF), jax.ShapeDtypeStruct((nt, 8, 128), F32)],
        in_specs=[vm] * len(args),
        out_specs=[vm, vm],
        scratch_shapes=[
            pltpu.VMEM((2, nt, CHUNK, 384), BF),
            pltpu.VMEM((NZ, ROWS * EMB, 2 * CHUNK), BF),
            pltpu.VMEM((2, ROWS * EMB, 384), F32),
            pltpu.VMEM((ROWS, EMB, 256), BF),
            pltpu.VMEM((4, CPAD, CELLS), BF),
            pltpu.VMEM((n, 128), F32),
            pltpu.VMEM((EMB, 2 * CHUNK), F32),
            pltpu.VMEM((nt, 8, 128), F32),
            pltpu.VMEM((nt, 8, 128), F32),
            pltpu.VMEM((8, 128), F32),
            pltpu.VMEM((nm, 8, 128), F32),
            pltpu.VMEM((8, 128), F32),
            dma((2, 23)), dma((2, 23)), dma((4, 16)), dma((4, 16)), dma((3, 16)), dma((3, 16)),
        ],
        compiler_params=pltpu.CompilerParams(
            collective_id=0, has_side_effects=True, vmem_limit_bytes=62 * 2**20),
        name="forecast",
    )(*args)


def mix_of(stats, n):
    rows = lax.broadcasted_iota(jnp.int32, (n, n), 0)
    cols = lax.broadcasted_iota(jnp.int32, (n, n), 1)
    eye = (rows == cols).astype(F32)
    rw = lax.broadcasted_iota(jnp.int32, (n, 128), 0)
    cw = lax.broadcasted_iota(jnp.int32, (n, 128), 1)
    wide = jnp.where(cw < n, stats / (n - 1.0) + (rw == cw).astype(F32), stats)
    system = wide[:, :n]
    scale = jnp.sqrt(jnp.sum(system * system))
    up, root = system / scale, eye
    done = 0
    for it in range(NS_ITERS):
        shift = 1.5 * eye - 0.5 * jnp.dot(root, up, precision=HI, preferred_element_type=F32)
        up = jnp.dot(up, shift, precision=HI, preferred_element_type=F32)
        root = jnp.dot(shift, root, precision=HI, preferred_element_type=F32)
        upto = min(n, -(-n * (it + 1) // NS_ITERS))
        for j in range(done, upto):
            r = wide[j:j + 1, :]
            r = r / wide[j:j + 1, j:j + 1]
            col = wide[:, j:j + 1] - (rw[:, :1] == j).astype(F32)
            wide = wide - col * r
        done = upto
    weight = wide[:, n:n + 1] / (n - 1.0)
    return root / jnp.sqrt(scale) + weight


def mix_kernel(stats_ref, mix_ref):
    mix_ref[...] = mix_of(stats_ref[...], mix_ref.shape[0])


def mix_call(stats, n):
    vm = pl.BlockSpec(memory_space=pltpu.VMEM)
    return pl.pallas_call(
        mix_kernel,
        out_shape=jax.ShapeDtypeStruct((n, n), F32),
        in_specs=[vm],
        out_specs=vm,
        name="mix",
    )(stats)


def update(patch, mix):
    base = patch.astype(F32)
    center = jnp.mean(base, axis=2, keepdims=True)
    moved = jnp.einsum("ckf,fn->ckn", base - center, mix, precision=HI)
    return (center + moved).astype(BF)


def shards(x, lift, gain, w1, w2, readout, obs_count, obs_cell, obs_op, obs_value, obs_error):
    mem, nvar, rows, nlon = x.shape
    nt, nm = lax.axis_size("tile"), lax.axis_size("member")
    n = mem * nm
    ncell = rows * nlon // nm
    fw, iv, lf, li = (jnp.asarray(a) for a in kernel_tables())
    xk = jnp.pad(x.reshape(mem, nvar, rows * nlon), ((0, 0), (0, CPAD - nvar), (0, CELLS - rows * nlon)))
    lt = lift.T
    one = jnp.concatenate([jnp.tile(lt[:, :64], (1, ROWS)), jnp.tile(lt[:, 64:], (1, ROWS)), jnp.zeros((EMB, 10), BF)], axis=1)
    lx = jnp.concatenate([one, one], axis=1)
    ltp = jnp.pad(lt, ((0, 0), (0, CPAD - nvar)))
    ro = jnp.pad(readout.T, ((0, CPAD - nvar), (0, 0)))
    gp = jnp.pad(gain, ((0, 0), (0, 128 - gain.shape[1])))
    args = (xk, fw, iv, lf, li, gp, lx, ltp, w1.T, w2.T, ro,
            obs_count.reshape(1, 1), obs_cell, obs_op[0], obs_value, obs_error)
    field, stats = forecast_call(args, nm, nt, n)
    stats = stats[:, : n // nt].reshape(n, 128)
    mix = mix_call(stats, n)
    patch = lax.dynamic_slice(field, (0, 0, 7 * lax.axis_index("member")), (n, nvar, ncell))
    return update(jnp.transpose(patch, (1, 2, 0)), mix)


def solution(mesh):
    placed = (
        P("member", None, "tile", None),
        P(), P(), P(), P(), P(),
        P(("tile", "member")),
        P(("tile", "member"), None),
        P(("tile", "member"), None, None),
        P(("tile", "member"), None),
        P(("tile", "member"), None),
    )
    return jax.shard_map(
        shards, mesh=mesh, in_specs=placed, out_specs=P(None, ("tile", "member"), None), check_vma=False)
```

time: 291 us -> 204 us (0.70)
  Pallas kernels: 35.4 us -> 152 us
  local copies, waits for them, and re-layouts: 118 us -> 32.7 us
  matrix products: 58.9 us -> 8.46 us
  waiting for transfers between devices: 31.5 us -> 0 us
  other arithmetic: 23.4 us -> 9.48 us
  between operations: 14.3 us -> 0.86 us
  starting transfers between devices: 7.89 us -> 0 us
    pallas_call x1, Pallas kernels: 25.2 us -> 141 us  [forecast_call(): pl.pallas_call(functools.partial(forecast_kernel, nm), out_shape=[jax.Sha...]
    mul x3 -> x0, local copies, waits for them, and re-layouts: 73.6 us -> none  [shards(): tr.reshape(rows, emb, nt, rows, 1)]
    dot_general x9 -> x0, matrix products: 51.3 us -> none  [the longest x1 24.5 us: shards(): jnp.dot(w, hats, preferred_element_type=F32).astype(BF)]
    all_to_all x1 -> x0, waiting for transfers between devices: 31.4 us -> none  [shards(): lax.all_to_all(lines, 'member', split_axis=1, concat_axis=3, tiled=True)]
    convert_element_type x3 -> x1, other arithmetic: 22.4 us -> 3.07 us  [update(): return (center + moved).astype(BF)]
    unnamed x30 -> x11, local copies, waits for them, and re-layouts: 18.2 us -> 6.98 us
    reshape x3 -> x2, local copies, waits for them, and re-layouts: 10.5 us -> 2.28 us  [shards(): x.reshape(mem, nvar, rows * nlon)]
    all_to_all x1 -> x0, starting transfers between devices: 7.89 us -> none  [shards(): lax.all_to_all(lines, 'member', split_axis=1, concat_axis=3, tiled=True)]
  transfers between devices with their start and end apart: 2 -> 0, of which waited for: 1 -> 0; matrix products, arithmetic and copies ran while one was open for 43% -> 0% of each run, Pallas kernels for 0% -> 0%
where the time goes in v2:
time: 204 us; the launch traced here: 203 us
  Pallas kernels  152 us (75%)
  local copies, waits for them, and re-layouts  32.7 us (16%)
  other arithmetic  9.48 us (5%)
  matrix products  8.46 us (4%)
    pallas_call x1, Pallas kernels, forecast_call(): pl.pallas_call(functools.partial(forecast_kernel, nm), out_shape=[jax.Sha...  141 us
    pallas_call x1, Pallas kernels, mix_call(): pl.pallas_call(mix_kernel, out_shape=jax.ShapeDtypeStruct((n, n), F32), i...  10.1 us
    dot_general x1, matrix products, update(): moved = jnp.einsum('ckf,fn->ckn', base - center, mix, precision=HI)  8.46 us
    unnamed x11, local copies, waits for them, and re-layouts  6.98 us
    dot_general x1, local copies, waits for them, and re-layouts, update(): moved = jnp.einsum('ckf,fn->ckn', base - center, mix, precision=HI)  6.39 us
    sub x1, local copies, waits for them, and re-layouts, update(): moved = jnp.einsum('ckf,fn->ckn', base - center, mix, precision=HI)  6.37 us

profile of v2, /device:TPU:1, one launch (start us, length us, event | category | flops | bytes accessed | tf_op | source)
XLA Modules:
  0.0 203.0 jit_solution(14436524569948665558)
XLA Ops:
  0.0 0.0 copy-start.1
  0.8 1.4 pad.19.ro_ref
  2.2 0.9 copy.46
  3.1 0.1 copy.47
  3.2 0.6 pad.18.lt_ref
  3.8 0.1 slice.13
  3.9 0.1 copy.48
  4.0 0.1 copy.50
  4.1 1.5 copy.55
  5.6 1.0 copy.45
  6.6 0.7 pad.17.gain_ref
  7.3 0.2 copy.49
  7.5 1.1 concatenate.5.lx_ref
  8.6 1.8 copy.53
  10.4 1.8 copy.54
  12.2 0.0 copy-done.1
  12.2 0.3 copy.61
  12.5 2.0 reshape.25
  14.5 1.2 pad.16.x_ref
  15.7 141.4 %forecast.1 = (bf16[64,80,256]{2,1,0:T(8,128)(2,1)}, f32[16,8,128]{2,1,0:T(8,128)}) custom-call(bf16[4,80,2304]{2,1,0:T(8,128)(2,1)} %pad.16.x_ref, bf16[6,512,256]{2,1,0:T(8,128)(2,1)} %constant.28.clone.fw_ref, bf16[9,512,256]{2,1,0:T(8,128)(2,1)} %constant.29.clone.iv_ref, bf16[8,256,896]{2,1,0:T(8,128)(2,1)} %constant.30.clone.lf_ref, ...), custom_call_target="tpu_custom_call" | custom-call | tf_op jit(solution)/shard_map/forecast/pallas_call | solution.py:367
  157.1 0.0 copy-start
  157.1 1.6 slice.11
  158.7 10.1 %mix.1 = f32[64,64]{1,0:T(8,128)} custom-call(f32[64,128]{1,0:T(8,128)} %bitcast.26), custom_call_target="tpu_custom_call" | custom-call | tf_op jit(solution)/shard_map/mix/pallas_call | solution.py:425
  168.9 2.8 %bitcast_reduce_fusion = f32[73,135]{1,0:T(8,128)S(1)} fusion(bf16[64,80,256]{2,1,0:T(8,128)(2,1)} %get-tuple-element.7, s32[]{:T(128)S(6)} %select_n.3), kind=kLoop, calls=%fused_computation.1 | loop fusion | flops 1251585 | bytes 1300864 | tf_op jit(solution)/shard_map/reduce_sum | solution.py:436
  171.7 0.0 copy-done
  171.7 3.6 %bitcast_subtract_fusion = f32[73,135,64]{1,0,2:T(8,128)} fusion(f32[73,135]{1,0:T(8,128)S(1)} %broadcast_multiply_fusion, bf16[64,80,256]{2,1,0:T(8,128)(2,1)S(1)} %copy-done, s32[]{:T(128)S(6)} %select_n.3), kind=kLoop, calls=%fused_computation | loop fusion | flops 1261440 | bytes 3823744 | tf_op jit(solution)/shard_map/sub | solution.py:437
  175.3 0.0 copy-start.2
  175.3 6.4 %copy.56 = f32[73,135,64]{0,2,1:T(8,128)} copy(f32[73,135,64]{1,0,2:T(8,128)} %bitcast_subtract_fusion) | data formatting | bytes 5045760 | tf_op jit(solution)/shard_map/sub | solution.py:437
  181.7 0.0 copy-done.2
  181.7 8.5 %fusion = f32[73,135,64]{0,2,1:T(8,128)} fusion(f32[73,135,64]{0,2,1:T(8,128)} %copy.56, f32[64,64]{1,0:T(8,128)S(1)} %copy-done.2), kind=kOutput, calls=%fused_computation.4 | convolution fusion | flops 484392960 | bytes 5062144 | tf_op jit(solution)/shard_map/ckf,fn->ckn/dot_general | solution.py:437
  190.1 6.4 %copy.58 = f32[73,135,64]{1,0,2:T(8,128)} copy(f32[73,135,64]{0,2,1:T(8,128)} %fusion) | data formatting | bytes 5045760 | tf_op jit(solution)/shard_map/ckf,fn->ckn/dot_general | solution.py:437
  196.5 3.1 %add_convert_fusion = bf16[73,135,64]{1,0,2:T(8,128)(2,1)S(1)} fusion(f32[73,135,64]{1,0,2:T(8,128)} %copy.58, f32[73,135]{1,0:T(8,128)S(1)} %broadcast_multiply_fusion), kind=kLoop, calls=%fused_computation.2 | loop fusion | flops 1261440 | bytes 3823740 | tf_op jit(solution)/shard_map/convert_element_type | solution.py:438
  199.6 3.4 %copy.59 = bf16[73,135,64]{0,2,1:T(8,128)(2,1)} copy(bf16[73,135,64]{1,0,2:T(8,128)(2,1)S(1)} %add_convert_fusion) | data formatting | bytes 2522880 | tf_op jit(solution)/shard_map/convert_element_type | solution.py:438
  (5 shorter events, 0.1 us)
Async XLA Ops:
  0.0 12.2 %copy-start.1 = (bf16[4,73,6,360]{3,0,2,1:T(4,128)(2,1)S(1)}, bf16[4,73,6,360]{3,0,2,1:T(4,128)(2,1)}, u32[]{:S(2)}) copy-start(bf16[4,73,6,360]{3,0,2,1:T(4,128)(2,1)} %param.15) | copy-start | bytes 3784324
  157.1 14.6 %copy-start = (bf16[64,80,256]{2,1,0:T(8,128)(2,1)S(1)}, bf16[64,80,256]{2,1,0:T(8,128)(2,1)}, u32[]{:S(2)}) copy-start(bf16[64,80,256]{2,1,0:T(8,128)(2,1)} %get-tuple-element.7) | copy-start | bytes 7864324
  175.3 6.4 %copy-start.2 = (f32[64,64]{1,0:T(8,128)S(1)}, f32[64,64]{1,0:T(8,128)}, u32[]{:S(2)}) copy-start(f32[64,64]{1,0:T(8,128)} %mix.1) | copy-start | bytes 49156

commit v3 on v2

--- a/solution.py
+++ b/solution.py
@@ -44,6 +44,7 @@
 CELLS = 2304
 EMB, HID = 256, 512
 NZ = 8
+NCELL = 135
 
 
 def chunk_index():
@@ -77,24 +78,23 @@
                 if 0 <= q < 360:
                     iv[n, s, :KCOL, col] = lon_i[:, q]
     lat, chan = chunk_index()
-    lf = np.zeros((16, 256, CHUNK), np.float32)
+    lf = np.zeros((16, NLAT, CHUNK), np.float32)
     for t in range(16):
-        cols = lat_f[:, 6 * t + np.maximum(lat, 0)] * (lat >= 0)
-        lf[t, :NLAT], lf[t, 128:128 + NLAT] = cols, cols
-    lf = lf.reshape(NZ, 2, 256, CHUNK).transpose(0, 2, 1, 3).reshape(NZ, 256, 2 * CHUNK)
-    li = np.zeros((NLAT, 128), np.float32)
-    li[:, :NLAT] = lat_i
-    return fw.astype(BF), iv.reshape(9, 512, 256).astype(BF), lf.astype(BF), li
+        lf[t] = lat_f[:, 6 * t + np.maximum(lat, 0)] * (lat >= 0)
+    lf = lf.reshape(NZ, 2, NLAT, CHUNK).transpose(0, 2, 1, 3).reshape(NZ, NLAT, 2 * CHUNK)
+    spread = (chan[None, :] == np.arange(VARS)[:, None]).astype(np.float32)
+    spread = np.concatenate([spread, spread], axis=1)
+    return fw.astype(BF), iv.reshape(9, 512, 256).astype(BF), lf.astype(BF), lat_i, spread.astype(BF)
 
 
 def dot(a, b):
     return jnp.dot(a, b, preferred_element_type=F32)
 
 
-def forecast_kernel(nm, x_ref, fw_ref, iv_ref, lf_ref, li_ref, gain_ref, lx_ref, lt_ref, w1_ref, w2_ref, ro_ref,
+def forecast_kernel(nm, x_ref, fw_ref, iv_ref, lf_ref, li_ref, sp_ref, gain_ref, lift_ref, w1_ref, w2_ref, ro_ref,
                     count_ref, cell_ref, op_ref, val_ref, err_ref,
-                    field_ref, stats_ref,
-                    spec, wmat, acc, bk, fs, cp, lx2, part, got, mid, midg, fin,
+                    ft_ref, stats_ref,
+                    spec, wmat, acc, bk, fs, field_ref, cp, lx, lt, w1t, w2t, rot, gt, turn, stage, part, got, mid, midg, fin,
                     ag_s, ag_r, ax_s, ax_r, rs_s, rs_r):
     m, t = lax.axis_index("member"), lax.axis_index("tile")
     nt = 2 * NZ
@@ -117,19 +117,37 @@
         pl.semaphore_signal(bar, inc=1, device_id=member_peer(i), device_id_type=MESH)
 
     low64 = lax.broadcasted_iota(jnp.int32, (CPAD, 128), 1) < 64
-
-    def spectra(q):
-        tails = []
+    low64e = lax.broadcasted_iota(jnp.int32, (EMB, 128), 1) < 64
+
+    def half_turn(v):
+        return pltpu.roll(v, 64, 1)
+
+    def spectra(pieces):
+        tails = {i: [] for i in pieces}
         for p in range(ROWS):
             at, wide = window(p)
-            v0 = dot(x_ref[2 * q, :, at:at + wide], fw_ref[p, :wide])
-            v1 = dot(x_ref[2 * q + 1, :, at:at + wide], fw_ref[p, :wide])
-            mixed = jnp.where(low64, v0[:, 128:], pltpu.roll(v1[:, 128:], 64, 1))
-            v = jnp.concatenate([v0[:, :128], mixed, v1[:, :128]], axis=1)
-            spec[q, t, 64 * p:64 * p + 64] = v[:64].astype(BF)
-            tails.append(v[64:VARS])
-        tails.append(jnp.zeros((10, 384), F32))
-        spec[q, t, 384:CHUNK] = jnp.concatenate(tails, axis=0).astype(BF)
+
+            def both(e):
+                v = dot(x_ref[e, :, at:at + wide], fw_ref[p, :wide])
+                return v[:, :128], v[:, 128:]
+
+            for i in pieces:
+                if i == 0:
+                    (a0, b0), (a1, _) = both(0), both(1)
+                    v = [a0, jnp.where(low64, b0, half_turn(a1))]
+                elif i == 1:
+                    (a1, b1), (a2, _) = both(1), both(2)
+                    v = [jnp.where(low64, half_turn(a1), half_turn(b1)), a2]
+                else:
+                    (_, b2), (a3, b3) = both(2), both(3)
+                    a3 = half_turn(a3)
+                    v = [jnp.where(low64, b2, a3), jnp.where(low64, a3, half_turn(b3))]
+                v = jnp.concatenate(v, axis=1)
+                spec[i, t, 64 * p:64 * p + 64] = v[:64].astype(BF)
+                tails[i].append(v[64:VARS])
+        for i in pieces:
+            tails[i].append(jnp.zeros((10, 256), F32))
+            spec[i, t, 384:CHUNK] = jnp.concatenate(tails[i], axis=0).astype(BF)
 
     sent = []
 
@@ -183,47 +201,51 @@
 
         @pl.loop(0, ROWS)
         def _(p):
-            g = gain_ref[...] * li_ref[pl.ds(ROWS * t + p, 1), :]
-            hi = g.astype(BF)
-            lo = (g - hi.astype(F32)).astype(BF)
-            w = dot(jnp.concatenate([hi, lo], axis=1), lf_ref[zz])
-            wmat[zz, pl.ds(pl.multiple_of(p * EMB, EMB), EMB), :] = (w * lx2[...]).astype(BF)
-
-    def apply(q, d):
-        zz = zat(d)
-        g = spec[q, pl.ds(zz * 2, 2)].reshape(2 * CHUNK, 384)
+            g = (gt[...] * li_ref[pl.ds(ROWS * t + p, 1), :]).astype(BF)
+            w = dot(g, lf_ref[zz]).astype(BF)
+            wmat[zz, pl.ds(pl.multiple_of(p * EMB, EMB), EMB), :] = w * lx[...]
+
+    def apply(i, d, e, first=False):
+        za, zb = zat(d), zat(e)
+        g = jnp.concatenate([spec[i, pl.ds(zz * 2, 2)].reshape(2 * CHUNK, 256) for zz in (za, zb)], axis=0)
 
         @pl.loop(0, 3)
         def _(b):
             rows = pl.ds(pl.multiple_of(b * 512, 512), 512)
-            v = dot(wmat[zz, rows, :], g)
-            acc[q, rows, :] = v if d == 0 else acc[q, rows, :] + v
+            v = dot(jnp.concatenate([wmat[za, rows, :], wmat[zb, rows, :]], axis=1), g)
+            acc[i, rows, :] = v if first else acc[i, rows, :] + v
 
     c0 = math.sqrt(2.0 / math.pi)
 
     def member(e):
-        q = e // 2
-
         @pl.loop(0, ROWS)
         def _(p):
-            a = acc[q, pl.ds(pl.multiple_of(p * EMB, EMB), EMB), :]
-            if e % 2:
-                a = jnp.concatenate([a[:, 256:], pltpu.roll(a[:, 128:256], 64, 1)], axis=1)
+            rows = pl.ds(pl.multiple_of(p * EMB, EMB), EMB)
+            if e == 0:
+                a = acc[0, rows, :]
+            elif e == 2:
+                a = jnp.concatenate([acc[1, rows, 128:], acc[2, rows, :128]], axis=1)
             else:
-                a = a[:, :256]
+                head = half_turn(acc[0, rows, 128:] if e == 1 else acc[2, rows, :128])
+                rest = half_turn(acc[1, rows, :128] if e == 1 else acc[2, rows, 128:])
+                a = jnp.concatenate([jnp.where(low64e, head, rest), rest], axis=1)
             bk[p] = a.astype(BF)
 
-        @pl.loop(0, 9)
-        def _(n):
-            low = jnp.minimum(256 * n // 360, 4)
-            lanes = pl.ds(pl.multiple_of(n * 256, 256), 256)
+        @pl.loop(0, 3)
+        def _(it):
+            lanes = pl.ds(pl.multiple_of(it * 768, 768), 768)
             x = x_ref[e, :, lanes]
-            s = dot(jnp.concatenate([bk[low], bk[low + 1]], axis=1), iv_ref[n])
-            mixed = (s + dot(lt_ref[...], x)).astype(BF)
-            u = dot(w1_ref[...], mixed)
-            u = 0.5 * u * (1.0 + jnp.tanh(c0 * (u + 0.044715 * (u * u * u))))
-            outer = (mixed.astype(F32) + dot(w2_ref[...], u.astype(BF))).astype(BF)
-            fs[e, :, lanes] = (x.astype(F32) + dot(ro_ref[...], outer)).astype(BF)
+            parts = []
+            for k in range(3):
+                n = 3 * it + k
+                low = jnp.minimum(256 * n // 360, 4)
+                parts.append(dot(jnp.concatenate([bk[low], bk[low + 1]], axis=1), iv_ref[n]))
+            mixed = (jnp.concatenate(parts, axis=1) + dot(lt[...], x)).astype(BF)
+            u = dot(w1t[...], mixed)
+            h = 0.5 * u
+            u = h * jnp.tanh(u * (c0 + (c0 * 0.044715) * (u * u))) + h
+            outer = (mixed.astype(F32) + dot(w2t[...], u.astype(BF))).astype(BF)
+            fs[e, :, lanes] = (x.astype(F32) + dot(rot[...], outer)).astype(BF)
 
         for i in range(1, nm):
             go(out_copy(e, i))
@@ -235,78 +257,96 @@
             src_ref=fs.at[e, :, pl.ds(pl.multiple_of(128 * to, 128), 256)], dst_ref=field_ref.at[4 * m + e],
             send_sem=ax_s.at[e, i], recv_sem=ax_r.at[e, i], device_id=(to, t), device_id_type=MESH)
 
-    spectra(0)
+    spectra((0,))
     pl.semaphore_wait(bar, nt + nm - 2)
     own(0)
-    spectra(1)
-    lx2[...] = lx_ref[...].astype(F32)
-    for d in (0, 1, -1):
-        weights(d)
+    spectra((1, 2))
+    lv = jnp.concatenate([lift_ref[...].astype(F32), jnp.zeros((CPAD - VARS, EMB), F32)], axis=0).T.astype(BF)
+    lt[...] = lv
+    lx[...] = dot(lv[:, :VARS], sp_ref[...]).astype(BF)
+    gt[...] = gain_ref[...].T
+    weights(1)
+    weights(-1)
     step(0, 1, 0)
     weights(2)
     step(0, 1, 1)
+    own(1)
     weights(-2)
-    from_sib(0, 0)
-    apply(0, 0)
     step(0, 2, 0)
     weights(3)
-    from_sib(0, 1)
-    apply(0, 1)
     step(0, 2, 1)
     weights(-3)
+    from_sib(0, 1)
     from_sib(0, -1)
-    apply(0, -1)
-    own(1)
+    apply(0, 1, -1, True)
     step(0, 3, 0)
-    weights(4)
+    weights(0)
+    step(0, 3, 1)
     from_sib(0, 2)
-    apply(0, 2)
-    step(0, 3, 1)
     from_sib(0, -2)
-    apply(0, -2)
+    apply(0, 2, -2)
     step(0, 4, 0)
     step(0, 4, 1)
-    from_sib(1, 0)
-    apply(1, 0)
+    weights(4)
+    step(1, 1, 0)
+    step(1, 1, 1)
+    own(2)
     from_sib(0, 3)
-    apply(0, 3)
-    step(1, 1, 0)
     from_sib(0, -3)
-    apply(0, -3)
-    step(1, 1, 1)
+    apply(0, 3, -3)
+    step(1, 2, 0)
+    from_sib(0, 0)
     from_sib(0, 4)
-    apply(0, 4)
-    step(1, 2, 0)
-    member(0)
+    apply(0, 0, 4)
     step(1, 2, 1)
+    w1t[...] = w1_ref[...].astype(F32).T.astype(BF)
+    w2t[...] = w2_ref[...].astype(F32).T.astype(BF)
+    rot[...] = jnp.concatenate([ro_ref[...].astype(F32), jnp.zeros((CPAD - VARS, EMB), F32)], axis=0).astype(BF)
     from_sib(1, 1)
-    apply(1, 1)
     from_sib(1, -1)
-    apply(1, -1)
+    apply(1, 1, -1, True)
     step(1, 3, 0)
-    member(1)
+    from_sib(1, 2)
+    from_sib(1, -2)
+    apply(1, 2, -2)
     step(1, 3, 1)
-    from_sib(1, 2)
-    apply(1, 2)
-    from_sib(1, -2)
-    apply(1, -2)
     step(1, 4, 0)
     step(1, 4, 1)
+    step(2, 1, 0)
+    member(0)
+    step(2, 1, 1)
     from_sib(1, 3)
-    apply(1, 3)
     from_sib(1, -3)
-    apply(1, -3)
+    apply(1, 3, -3)
+    step(2, 2, 0)
+    from_sib(1, 0)
     from_sib(1, 4)
-    apply(1, 4)
+    apply(1, 0, 4)
+    step(2, 2, 1)
+    from_sib(2, 1)
+    from_sib(2, -1)
+    apply(2, 1, -1, True)
+    step(2, 3, 0)
+    step(2, 3, 1)
+    member(1)
+    step(2, 4, 0)
+    step(2, 4, 1)
+    from_sib(2, 2)
+    from_sib(2, -2)
+    apply(2, 2, -2)
+    from_sib(2, 3)
+    from_sib(2, -3)
+    apply(2, 3, -3)
+    from_sib(2, 0)
+    from_sib(2, 4)
+    apply(2, 0, 4)
     member(2)
     member(3)
 
     cells = cell_ref[...] + 7 * m
     pick = (lax.broadcasted_iota(jnp.int32, (256, 128), 0) == cells).astype(BF)
-    ident = (lax.broadcasted_iota(jnp.int32, (CPAD, VARS), 0)
-             == lax.broadcasted_iota(jnp.int32, (CPAD, VARS), 1)).astype(F32)
     nt_dims = (((1,), (1,)), ((), ()))
-    op = lax.dot_general(ident, op_ref[...], nt_dims, precision=HI, preferred_element_type=F32)
+    op = jnp.concatenate([op_ref[...].reshape(VARS, 128), jnp.zeros((CPAD - VARS, 128), F32)], axis=0)
 
     def counterparts(e, src):
         f = 4 * src + e
@@ -338,7 +378,18 @@
         go(cc)
         return cc
 
+    def turned(g):
+        @pl.loop(0, 16)
+        def _(k):
+            turn[k, :, :CPAD] = field_ref[16 * g + k].astype(F32).T
+
+        for hf in range(2):
+            v = turn[8 * hf:8 * hf + 8, pl.ds(7 * m, NCELL), :]
+            stage[:, 8 * hf:8 * hf + 8, :] = jnp.transpose(v, (1, 0, 2))
+        ft_ref[:, 16 * g:16 * g + 16, :] = stage[...].astype(BF)
+
     one = [send(part.at[lax.rem(t + i, nt)], got.at[i], 0, i, tile_peer(i)) for i in range(1, nt)]
+    turned(0)
     tot = part[t]
     for cc in one:
         cc.wait_recv()
@@ -347,6 +398,7 @@
     mid[...] = tot
     two = [send(mid, midg.at[m], 1, i, member_peer(i)) for i in range(1, nm)]
     midg[m] = tot
+    turned(1)
     for cc in two:
         cc.wait_recv()
     tot = midg[0]
@@ -355,6 +407,8 @@
     stats_ref[t] = tot
     fin[...] = tot
     three = [send(fin, stats_ref.at[t], 2, i, tile_peer(i)) for i in range(1, nt)]
+    turned(2)
+    turned(3)
     for cc in three:
         cc.wait_recv()
     for cc in sent:
@@ -366,23 +420,31 @@
     dma = pltpu.SemaphoreType.DMA
     return pl.pallas_call(
         functools.partial(forecast_kernel, nm),
-        out_shape=[jax.ShapeDtypeStruct((n, CPAD, 256), BF), jax.ShapeDtypeStruct((nt, 8, 128), F32)],
+        out_shape=[jax.ShapeDtypeStruct((NCELL, n, 128), BF), jax.ShapeDtypeStruct((nt, 8, 128), F32)],
         in_specs=[vm] * len(args),
         out_specs=[vm, vm],
         scratch_shapes=[
-            pltpu.VMEM((2, nt, CHUNK, 384), BF),
+            pltpu.VMEM((3, nt, CHUNK, 256), BF),
             pltpu.VMEM((NZ, ROWS * EMB, 2 * CHUNK), BF),
-            pltpu.VMEM((2, ROWS * EMB, 384), F32),
+            pltpu.VMEM((3, ROWS * EMB, 256), F32),
             pltpu.VMEM((ROWS, EMB, 256), BF),
             pltpu.VMEM((4, CPAD, CELLS), BF),
+            pltpu.VMEM((n, CPAD, 256), BF),
             pltpu.VMEM((n, 128), F32),
-            pltpu.VMEM((EMB, 2 * CHUNK), F32),
+            pltpu.VMEM((EMB, 2 * CHUNK), BF),
+            pltpu.VMEM((EMB, CPAD), BF),
+            pltpu.VMEM((HID, EMB), BF),
+            pltpu.VMEM((EMB, HID), BF),
+            pltpu.VMEM((CPAD, EMB), BF),
+            pltpu.VMEM((EMB, NLAT), F32),
+            pltpu.VMEM((16, 256, 128), F32),
+            pltpu.VMEM((NCELL, 16, 128), F32),
             pltpu.VMEM((nt, 8, 128), F32),
             pltpu.VMEM((nt, 8, 128), F32),
             pltpu.VMEM((8, 128), F32),
             pltpu.VMEM((nm, 8, 128), F32),
             pltpu.VMEM((8, 128), F32),
-            dma((2, 23)), dma((2, 23)), dma((4, 16)), dma((4, 16)), dma((3, 16)), dma((3, 16)),
+            dma((3, 23)), dma((3, 23)), dma((4, 16)), dma((4, 16)), dma((3, 16)), dma((3, 16)),
         ],
         compiler_params=pltpu.CompilerParams(
             collective_id=0, has_side_effects=True, vmem_limit_bytes=62 * 2**20),
@@ -416,48 +478,56 @@
     return root / jnp.sqrt(scale) + weight
 
 
-def mix_kernel(stats_ref, mix_ref):
-    mix_ref[...] = mix_of(stats_ref[...], mix_ref.shape[0])
-
-
-def mix_call(stats, n):
+def analysis_kernel(stats_ref, ft_ref, out_ref, dev, mean):
+    n = ft_ref.shape[1]
+    nt = stats_ref.shape[0]
+    step = 9
+
+    @pl.loop(0, NCELL // step)
+    def _(i):
+        for k in range(step):
+            v = ft_ref[i * step + k].astype(F32)
+            bar = jnp.mean(v, axis=0, keepdims=True)
+            mean[i * step + k] = bar
+            dev[i * step + k] = (v - bar).astype(BF)
+
+    stats = jnp.concatenate([stats_ref[b, :n // nt] for b in range(nt)], axis=0)
+    mix = mix_of(stats, n).T
+    hi = mix.astype(BF)
+    lo = (mix - hi.astype(F32)).astype(BF)
+    both = jnp.concatenate([hi, lo], axis=1)
+
+    @pl.loop(0, NCELL // step)
+    def _(i):
+        d = jnp.concatenate([dev[i * step + k] for k in range(step)], axis=1)
+        v = dot(both, jnp.concatenate([d, d], axis=0))
+        for k in range(step):
+            out_ref[i * step + k] = (v[:, 128 * k:128 * k + VARS] + mean[i * step + k][:, :VARS]).astype(BF)
+
+
+def analysis_call(stats, ft):
     vm = pl.BlockSpec(memory_space=pltpu.VMEM)
+    n = ft.shape[1]
     return pl.pallas_call(
-        mix_kernel,
-        out_shape=jax.ShapeDtypeStruct((n, n), F32),
-        in_specs=[vm],
+        analysis_kernel,
+        out_shape=jax.ShapeDtypeStruct((NCELL, n, VARS), BF),
+        in_specs=[vm, vm],
         out_specs=vm,
-        name="mix",
-    )(stats)
-
-
-def update(patch, mix):
-    base = patch.astype(F32)
-    center = jnp.mean(base, axis=2, keepdims=True)
-    moved = jnp.einsum("ckf,fn->ckn", base - center, mix, precision=HI)
-    return (center + moved).astype(BF)
+        scratch_shapes=[pltpu.VMEM((NCELL, n, 128), BF), pltpu.VMEM((NCELL, 1, 128), F32)],
+        compiler_params=pltpu.CompilerParams(vmem_limit_bytes=40 * 2**20),
+        name="analysis",
+    )(stats, ft)
 
 
 def shards(x, lift, gain, w1, w2, readout, obs_count, obs_cell, obs_op, obs_value, obs_error):
     mem, nvar, rows, nlon = x.shape
     nt, nm = lax.axis_size("tile"), lax.axis_size("member")
-    n = mem * nm
-    ncell = rows * nlon // nm
-    fw, iv, lf, li = (jnp.asarray(a) for a in kernel_tables())
+    tables = (jnp.asarray(a) for a in kernel_tables())
     xk = jnp.pad(x.reshape(mem, nvar, rows * nlon), ((0, 0), (0, CPAD - nvar), (0, CELLS - rows * nlon)))
-    lt = lift.T
-    one = jnp.concatenate([jnp.tile(lt[:, :64], (1, ROWS)), jnp.tile(lt[:, 64:], (1, ROWS)), jnp.zeros((EMB, 10), BF)], axis=1)
-    lx = jnp.concatenate([one, one], axis=1)
-    ltp = jnp.pad(lt, ((0, 0), (0, CPAD - nvar)))
-    ro = jnp.pad(readout.T, ((0, CPAD - nvar), (0, 0)))
-    gp = jnp.pad(gain, ((0, 0), (0, 128 - gain.shape[1])))
-    args = (xk, fw, iv, lf, li, gp, lx, ltp, w1.T, w2.T, ro,
-            obs_count.reshape(1, 1), obs_cell, obs_op[0], obs_value, obs_error)
-    field, stats = forecast_call(args, nm, nt, n)
-    stats = stats[:, : n // nt].reshape(n, 128)
-    mix = mix_call(stats, n)
-    patch = lax.dynamic_slice(field, (0, 0, 7 * lax.axis_index("member")), (n, nvar, ncell))
-    return update(jnp.transpose(patch, (1, 2, 0)), mix)
+    args = (xk, *tables, gain.T, lift, w1, w2, readout.T,
+            obs_count.reshape(1, 1), obs_cell, obs_op.transpose(2, 0, 1), obs_value, obs_error)
+    ft, stats = forecast_call(args, nm, nt, mem * nm)
+    return jnp.transpose(analysis_call(stats, ft), (2, 0, 1))
 
 
 def solution(mesh):

time: 204 us -> 150 us (0.74)
  local copies, waits for them, and re-layouts: 32.7 us -> 7.28 us
  Pallas kernels: 152 us -> 142 us
  other arithmetic: 9.48 us -> 0 us
  matrix products: 8.46 us -> 0 us
    pallas_call x1, Pallas kernels: 141 us -> 128 us  [forecast_call(): pl.pallas_call(functools.partial(forecast_kernel, nm), out_shape=[jax.Sha...]
    dot_general x1 -> x0, matrix products: 8.46 us -> none  [update(): moved = jnp.einsum('ckf,fn->ckn', base - center, mix, precision=HI)]
    dot_general x1 -> x0, local copies, waits for them, and re-layouts: 6.39 us -> none  [update(): moved = jnp.einsum('ckf,fn->ckn', base - center, mix, precision=HI)]
    sub x1 -> x0, local copies, waits for them, and re-layouts: 6.37 us -> none  [update(): moved = jnp.einsum('ckf,fn->ckn', base - center, mix, precision=HI)]
    unnamed x11 -> x4, local copies, waits for them, and re-layouts: 6.98 us -> 2.46 us
    pallas_call x1, Pallas kernels: 10.1 us -> 14.2 us  [analysis_call(): pl.pallas_call(analysis_kernel, out_shape=jax.ShapeDtypeStruct((NCELL, n,...]
    sub x1 -> x0, other arithmetic: 3.56 us -> none  [update(): moved = jnp.einsum('ckf,fn->ckn', base - center, mix, precision=HI)]
    convert_element_type x1 -> x0, local copies, waits for them, and re-layouts: 3.4 us -> none  [update(): return (center + moved).astype(BF)]
where the time goes in v3:
time: 150 us
  Pallas kernels  142 us (95%)
  local copies, waits for them, and re-layouts  7.28 us (5%)
    pallas_call x1, Pallas kernels, forecast_call(): pl.pallas_call(functools.partial(forecast_kernel, nm), out_shape=[jax.Sha...  128 us
    pallas_call x1, Pallas kernels, analysis_call(): pl.pallas_call(analysis_kernel, out_shape=jax.ShapeDtypeStruct((NCELL, n,...  14.2 us
    reshape x2, local copies, waits for them, and re-layouts, shards(): x.reshape(mem, nvar, rows * nlon)  3.61 us

profile of v3, /device:TPU:1, one launch (start us, length us, event | category | flops | bytes accessed | tf_op | source)
XLA Modules:
  0.0 150.0 jit_solution(6051640588461438134)
XLA Ops:
  0.7 1.6 %copy.20 = bf16[4,73,6,360]{3,2,1,0:T(8,128)(2,1)S(1)} copy(bf16[4,73,6,360]{3,0,2,1:T(4,128)(2,1)} %param.16) | data formatting | bytes 2522880 | tf_op jit(solution)/shard_map/reshape | solution.py:526
  2.3 2.0 %reshape.8 = bf16[4,73,2160]{2,1,0:T(8,128)(2,1)S(1)} reshape(bf16[4,73,6,360]{3,2,1,0:T(8,128)(2,1)S(1)} %copy.20) | data formatting | bytes 2522880 | tf_op jit(solution)/shard_map/reshape | solution.py:526
  4.3 1.2 pad.4.x_ref
  5.5 127.9 %forecast.1 = (bf16[135,64,128]{2,1,0:T(8,128)(2,1)}, f32[16,8,128]{2,1,0:T(8,128)}) custom-call(bf16[4,80,2304]{2,1,0:T(8,128)(2,1)} %pad.4.x_ref, bf16[6,512,256]{2,1,0:T(8,128)(2,1)} %constant.13.clone.fw_ref, bf16[9,512,256]{2,1,0:T(8,128)(2,1)} %constant.14.clone.iv_ref, bf16[8,96,896]{2,1,0:T(8,128)(2,1)} %constant.15.clone.lf_ref, ...), custom_call_target="tpu_custom_call" | custom-call | tf_op jit(solution)/shard_map/forecast/pallas_call | solution.py:421
  133.4 0.0 copy-start
  133.4 1.6 %copy-done = bf16[135,64,128]{2,1,0:T(8,128)(2,1)S(1)} copy-done((bf16[135,64,128]{2,1,0:T(8,128)(2,1)S(1)}, bf16[135,64,128]{2,1,0:T(8,128)(2,1)}, u32[]{:S(2)}) %copy-start) | copy-done | bytes 2211864
  135.0 0.0 copy-start.1
  135.0 0.8 copy-done.1
  135.8 14.2 %analysis.1 = bf16[135,64,73]{2,1,0:T(8,128)(2,1)} custom-call(f32[16,8,128]{2,1,0:T(8,128)S(1)} %copy-done.1, bf16[135,64,128]{2,1,0:T(8,128)(2,1)S(1)} %copy-done), custom_call_target="tpu_custom_call" | custom-call | tf_op jit(solution)/shard_map/analysis/pallas_call | solution.py:511
Async XLA Ops:
  133.4 1.6 %copy-start = (bf16[135,64,128]{2,1,0:T(8,128)(2,1)S(1)}, bf16[135,64,128]{2,1,0:T(8,128)(2,1)}, u32[]{:S(2)}) copy-start(bf16[135,64,128]{2,1,0:T(8,128)(2,1)} %get-tuple-element.8.ft_ref) | copy-start | bytes 6635524
  135.0 0.8 copy-start.1

commit v4 on v3

--- a/solution.py
+++ b/solution.py
@@ -151,11 +151,9 @@
 
     sent = []
 
-    def half(h):
-        return pl.ds(0, CHUNK) if h is None else pl.ds(h * (CHUNK // 2), CHUNK // 2)
-
     def copy(q, dz, other, h, sem, dev):
-        ref = spec.at[q, zat(dz) * 2 + (1 - core if other else core), half(h)]
+        rows = pl.ds(0, CHUNK) if h is None else pl.ds(h * (CHUNK // 2), CHUNK // 2)
+        ref = spec.at[q, zat(dz) * 2 + (1 - core if other else core), rows]
         return pltpu.make_async_remote_copy(
             src_ref=ref, dst_ref=ref, send_sem=ag_s.at[q, sem], recv_sem=ag_r.at[q, sem],
             device_id=dev, device_id_type=MESH)
@@ -165,36 +163,26 @@
         sent.append(c)
 
     def own(q):
-        for h in range(2):
-            go(copy(q, 0, False, h, h, right))
-            go(copy(q, 0, False, h, 7 + h, left))
-        go(copy(q, 0, False, None, 14, sib))
-
-    def step(q, d, h):
-        if d < 4 or h == 0:
-            copy(q, -d, False, h, 2 * (d - 1) + h, right).wait_recv()
-            if d < 3 or (d == 3 and h == 0):
-                go(copy(q, -d, False, h, 2 * d + h, right))
-        if d < 4 or h == 1:
-            copy(q, d, False, h, 7 + (2 * (d - 1) + h if d < 4 else 6), left).wait_recv()
-            if d < 3 or (d == 3 and h == 1):
-                go(copy(q, d, False, h, 7 + (2 * d + h if d < 3 else 6), left))
-        if d == 4:
-            go(copy(q, 4, False, h, 21 + h, sib))
-        elif h == 1:
-            go(copy(q, -d, False, None, 14 + d, sib))
-            go(copy(q, d, False, None, 17 + d, sib))
+        go(copy(q, 0, False, None, 0, right))
+        go(copy(q, 0, False, None, 4, left))
+        go(copy(q, 0, False, None, 8, sib))
+
+    def step(q, d):
+        for sign, base, h, dev in ((-1, 0, 0, right), (1, 4, 1, left)):
+            copy(q, sign * d, False, h if d == 4 else None, base + d - 1, dev).wait_recv()
+            if d < 4:
+                go(copy(q, sign * d, False, h if d == 3 else None, base + d, dev))
+        for sign, base, h in ((-1, 8, 0), (1, 12, 1)):
+            go(copy(q, sign * d, False, h if d == 4 else None, base + d, sib))
 
     def from_sib(q, d):
         if d == 0:
-            copy(q, 0, True, None, 14, sib).wait_recv()
+            copy(q, 0, True, None, 8, sib).wait_recv()
         elif d == 4:
-            copy(q, 4, True, 0, 21, sib).wait_recv()
-            copy(q, 4, True, 1, 22, sib).wait_recv()
-        elif d < 0:
-            copy(q, d, True, None, 14 - d, sib).wait_recv()
+            copy(q, 4, True, 0, 12, sib).wait_recv()
+            copy(q, 4, True, 1, 16, sib).wait_recv()
         else:
-            copy(q, d, True, None, 17 + d, sib).wait_recv()
+            copy(q, d, True, None, 8 - d if d < 0 else 12 + d, sib).wait_recv()
 
     def weights(d):
         zz = zat(d)
@@ -249,91 +237,80 @@
 
         for i in range(1, nm):
             go(out_copy(e, i))
-        field_ref[4 * m + e] = fs[e, :, pl.ds(pl.multiple_of(128 * m, 128), 256)]
+        field_ref[nm * e + m] = fs[e, :, pl.ds(pl.multiple_of(128 * m, 128), 256)]
 
     def out_copy(e, i):
         to = lax.rem(m + i, nm)
         return pltpu.make_async_remote_copy(
-            src_ref=fs.at[e, :, pl.ds(pl.multiple_of(128 * to, 128), 256)], dst_ref=field_ref.at[4 * m + e],
+            src_ref=fs.at[e, :, pl.ds(pl.multiple_of(128 * to, 128), 256)], dst_ref=field_ref.at[nm * e + m],
             send_sem=ax_s.at[e, i], recv_sem=ax_r.at[e, i], device_id=(to, t), device_id_type=MESH)
 
     spectra((0,))
     pl.semaphore_wait(bar, nt + nm - 2)
     own(0)
-    spectra((1, 2))
+    spectra((1,))
+    own(1)
+    spectra((2,))
     lv = jnp.concatenate([lift_ref[...].astype(F32), jnp.zeros((CPAD - VARS, EMB), F32)], axis=0).T.astype(BF)
     lt[...] = lv
     lx[...] = dot(lv[:, :VARS], sp_ref[...]).astype(BF)
     gt[...] = gain_ref[...].T
     weights(1)
     weights(-1)
-    step(0, 1, 0)
     weights(2)
-    step(0, 1, 1)
-    own(1)
     weights(-2)
-    step(0, 2, 0)
+    step(0, 1)
     weights(3)
-    step(0, 2, 1)
+    step(1, 1)
     weights(-3)
+    weights(0)
     from_sib(0, 1)
     from_sib(0, -1)
     apply(0, 1, -1, True)
-    step(0, 3, 0)
-    weights(0)
-    step(0, 3, 1)
+    step(0, 2)
+    own(2)
+    weights(4)
+    from_sib(1, 1)
+    from_sib(1, -1)
+    apply(1, 1, -1, True)
+    step(1, 2)
     from_sib(0, 2)
     from_sib(0, -2)
     apply(0, 2, -2)
-    step(0, 4, 0)
-    step(0, 4, 1)
-    weights(4)
-    step(1, 1, 0)
-    step(1, 1, 1)
-    own(2)
+    step(0, 3)
+    from_sib(1, 2)
+    from_sib(1, -2)
+    apply(1, 2, -2)
+    step(2, 1)
+    w1t[...] = w1_ref[...].astype(F32).T.astype(BF)
+    w2t[...] = w2_ref[...].astype(F32).T.astype(BF)
+    rot[...] = jnp.concatenate([ro_ref[...].astype(F32), jnp.zeros((CPAD - VARS, EMB), F32)], axis=0).astype(BF)
+    step(1, 3)
     from_sib(0, 3)
     from_sib(0, -3)
     apply(0, 3, -3)
-    step(1, 2, 0)
+    step(0, 4)
+    from_sib(1, 3)
+    from_sib(1, -3)
+    apply(1, 3, -3)
+    step(1, 4)
     from_sib(0, 0)
     from_sib(0, 4)
     apply(0, 0, 4)
-    step(1, 2, 1)
-    w1t[...] = w1_ref[...].astype(F32).T.astype(BF)
-    w2t[...] = w2_ref[...].astype(F32).T.astype(BF)
-    rot[...] = jnp.concatenate([ro_ref[...].astype(F32), jnp.zeros((CPAD - VARS, EMB), F32)], axis=0).astype(BF)
-    from_sib(1, 1)
-    from_sib(1, -1)
-    apply(1, 1, -1, True)
-    step(1, 3, 0)
-    from_sib(1, 2)
-    from_sib(1, -2)
-    apply(1, 2, -2)
-    step(1, 3, 1)
-    step(1, 4, 0)
-    step(1, 4, 1)
-    step(2, 1, 0)
+    step(2, 2)
     member(0)
-    step(2, 1, 1)
-    from_sib(1, 3)
-    from_sib(1, -3)
-    apply(1, 3, -3)
-    step(2, 2, 0)
+    from_sib(2, 1)
+    from_sib(2, -1)
+    apply(2, 1, -1, True)
+    step(2, 3)
     from_sib(1, 0)
     from_sib(1, 4)
     apply(1, 0, 4)
-    step(2, 2, 1)
-    from_sib(2, 1)
-    from_sib(2, -1)
-    apply(2, 1, -1, True)
-    step(2, 3, 0)
-    step(2, 3, 1)
-    member(1)
-    step(2, 4, 0)
-    step(2, 4, 1)
     from_sib(2, 2)
     from_sib(2, -2)
     apply(2, 2, -2)
+    step(2, 4)
+    member(1)
     from_sib(2, 3)
     from_sib(2, -3)
     apply(2, 3, -3)
@@ -349,15 +326,33 @@
     op = jnp.concatenate([op_ref[...].reshape(VARS, 128), jnp.zeros((CPAD - VARS, 128), F32)], axis=0)
 
     def counterparts(e, src):
-        f = 4 * src + e
+        f = nm * e + src
         v = dot(field_ref[f], pick) * op
         cp[pl.ds(f, 1), :] = jnp.sum(v, axis=0, keepdims=True)
 
-    for e in range(4):
+    def turned(g):
+        @pl.loop(0, 16)
+        def _(k):
+            turn[k, :, :CPAD] = field_ref[16 * g + k].astype(F32).T
+
+        for hf in range(2):
+            v = turn[8 * hf:8 * hf + 8, pl.ds(7 * m, NCELL), :]
+            stage[:, 8 * hf:8 * hf + 8, :] = jnp.transpose(v, (1, 0, 2))
+        ft_ref[:, 16 * g:16 * g + 16, :] = stage[...].astype(BF)
+
+    def collect(e):
         for i in range(nm):
             if i:
                 out_copy(e, i).wait_recv()
             counterparts(e, lax.rem(m - i + nm, nm))
+
+    for e in range(3):
+        collect(e)
+        turned(e)
+    for cc in sent:
+        cc.wait_send()
+    sent.clear()
+    collect(3)
     c = cp[...]
     n = c.shape[0]
     ybar = jnp.mean(c, axis=0, keepdims=True)
@@ -378,18 +373,8 @@
         go(cc)
         return cc
 
-    def turned(g):
-        @pl.loop(0, 16)
-        def _(k):
-            turn[k, :, :CPAD] = field_ref[16 * g + k].astype(F32).T
-
-        for hf in range(2):
-            v = turn[8 * hf:8 * hf + 8, pl.ds(7 * m, NCELL), :]
-            stage[:, 8 * hf:8 * hf + 8, :] = jnp.transpose(v, (1, 0, 2))
-        ft_ref[:, 16 * g:16 * g + 16, :] = stage[...].astype(BF)
-
     one = [send(part.at[lax.rem(t + i, nt)], got.at[i], 0, i, tile_peer(i)) for i in range(1, nt)]
-    turned(0)
+    turned(3)
     tot = part[t]
     for cc in one:
         cc.wait_recv()
@@ -398,7 +383,6 @@
     mid[...] = tot
     two = [send(mid, midg.at[m], 1, i, member_peer(i)) for i in range(1, nm)]
     midg[m] = tot
-    turned(1)
     for cc in two:
         cc.wait_recv()
     tot = midg[0]
@@ -407,8 +391,6 @@
     stats_ref[t] = tot
     fin[...] = tot
     three = [send(fin, stats_ref.at[t], 2, i, tile_peer(i)) for i in range(1, nt)]
-    turned(2)
-    turned(3)
     for cc in three:
         cc.wait_recv()
     for cc in sent:
@@ -444,7 +426,7 @@
             pltpu.VMEM((8, 128), F32),
             pltpu.VMEM((nm, 8, 128), F32),
             pltpu.VMEM((8, 128), F32),
-            dma((3, 23)), dma((3, 23)), dma((4, 16)), dma((4, 16)), dma((3, 16)), dma((3, 16)),
+            dma((3, 17)), dma((3, 17)), dma((4, 16)), dma((4, 16)), dma((3, 16)), dma((3, 16)),
         ],
         compiler_params=pltpu.CompilerParams(
             collective_id=0, has_side_effects=True, vmem_limit_bytes=62 * 2**20),
@@ -452,21 +434,39 @@
     )(*args)
 
 
+def split(a):
+    hi = a.astype(BF)
+    rest = a - hi.astype(F32)
+    mid = rest.astype(BF)
+    return hi, mid, (rest - mid.astype(F32)).astype(BF)
+
+
 def mix_of(stats, n):
-    rows = lax.broadcasted_iota(jnp.int32, (n, n), 0)
-    cols = lax.broadcasted_iota(jnp.int32, (n, n), 1)
-    eye = (rows == cols).astype(F32)
     rw = lax.broadcasted_iota(jnp.int32, (n, 128), 0)
     cw = lax.broadcasted_iota(jnp.int32, (n, 128), 1)
-    wide = jnp.where(cw < n, stats / (n - 1.0) + (rw == cw).astype(F32), stats)
-    system = wide[:, :n]
-    scale = jnp.sqrt(jnp.sum(system * system))
+    low = cw < n
+    wide = jnp.where(low, stats / (n - 1.0) + (rw == cw).astype(F32), stats)
+    eye = ((rw == cw) | (rw + n == cw)).astype(F32)
+    system = jnp.where(low, wide, pltpu.roll(wide, n, 1))
+    scale = jnp.sqrt(0.5 * jnp.sum(system * system))
+
+    def left(parts):
+        hi, mid, lo = (v.astype(F32) for v in parts)
+        return jnp.concatenate(
+            [parts[0], jnp.where(low, mid, hi).astype(BF), jnp.where(low, lo, mid).astype(BF)], axis=1)
+
+    def right(parts):
+        hi, mid, lo = parts
+        return jnp.concatenate([hi, mid, hi, lo, hi, mid], axis=0)
+
     up, root = system / scale, eye
     done = 0
     for it in range(NS_ITERS):
-        shift = 1.5 * eye - 0.5 * jnp.dot(root, up, precision=HI, preferred_element_type=F32)
-        up = jnp.dot(up, shift, precision=HI, preferred_element_type=F32)
-        root = jnp.dot(shift, root, precision=HI, preferred_element_type=F32)
+        su, sr = split(up), split(root)
+        shift = 1.5 * eye - 0.5 * dot(left(sr), right(su))
+        ss = split(shift)
+        up = dot(left(su), right(ss))
+        root = dot(left(ss), right(sr))
         upto = min(n, -(-n * (it + 1) // NS_ITERS))
         for j in range(done, upto):
             r = wide[j:j + 1, :]
@@ -475,34 +475,32 @@
             wide = wide - col * r
         done = upto
     weight = wide[:, n:n + 1] / (n - 1.0)
-    return root / jnp.sqrt(scale) + weight
-
-
-def analysis_kernel(stats_ref, ft_ref, out_ref, dev, mean):
-    n = ft_ref.shape[1]
+    return root[:, :n] / jnp.sqrt(scale) + weight
+
+
+def analysis_kernel(stats_ref, field_ref, out_ref, ft, sem):
+    n = ft.shape[1]
     nt = stats_ref.shape[0]
+    load = pltpu.make_async_copy(field_ref, ft, sem)
+    load.start()
+    stats = jnp.concatenate([stats_ref[b, :n // nt] for b in range(nt)], axis=0)
+    mix = mix_of(stats, n)
+    mix = (mix + (1.0 - jnp.sum(mix, axis=0, keepdims=True)) / n).T
+    hi = mix.astype(BF)
+    lo = (mix - hi.astype(F32)).astype(BF)
+    rows = lax.broadcasted_iota(jnp.int32, (n, n), 0)
+    cols = lax.broadcasted_iota(jnp.int32, (n, n), 1)
+    order = (cols == (n // 4) * (rows & 3) + (rows >> 2)).astype(BF)
+    both = dot(order, jnp.concatenate([hi, lo], axis=1)).astype(BF)
+    load.wait()
     step = 9
 
     @pl.loop(0, NCELL // step)
     def _(i):
+        f = jnp.concatenate([ft[i * step + k] for k in range(step)], axis=1)
+        v = dot(both, jnp.concatenate([f, f], axis=0))
         for k in range(step):
-            v = ft_ref[i * step + k].astype(F32)
-            bar = jnp.mean(v, axis=0, keepdims=True)
-            mean[i * step + k] = bar
-            dev[i * step + k] = (v - bar).astype(BF)
-
-    stats = jnp.concatenate([stats_ref[b, :n // nt] for b in range(nt)], axis=0)
-    mix = mix_of(stats, n).T
-    hi = mix.astype(BF)
-    lo = (mix - hi.astype(F32)).astype(BF)
-    both = jnp.concatenate([hi, lo], axis=1)
-
-    @pl.loop(0, NCELL // step)
-    def _(i):
-        d = jnp.concatenate([dev[i * step + k] for k in range(step)], axis=1)
-        v = dot(both, jnp.concatenate([d, d], axis=0))
-        for k in range(step):
-            out_ref[i * step + k] = (v[:, 128 * k:128 * k + VARS] + mean[i * step + k][:, :VARS]).astype(BF)
+            out_ref[i * step + k] = v[:, 128 * k:128 * k + VARS].astype(BF)
 
 
 def analysis_call(stats, ft):
@@ -511,9 +509,9 @@
     return pl.pallas_call(
         analysis_kernel,
         out_shape=jax.ShapeDtypeStruct((NCELL, n, VARS), BF),
-        in_specs=[vm, vm],
+        in_specs=[vm, pl.BlockSpec(memory_space=pl.ANY)],
         out_specs=vm,
-        scratch_shapes=[pltpu.VMEM((NCELL, n, 128), BF), pltpu.VMEM((NCELL, 1, 128), F32)],
+        scratch_shapes=[pltpu.VMEM((NCELL, n, 128), BF), pltpu.SemaphoreType.DMA],
         compiler_params=pltpu.CompilerParams(vmem_limit_bytes=40 * 2**20),
         name="analysis",
     )(stats, ft)

time: 150 us -> 149 us (level)
  Pallas kernels: 142 us -> 140 us
    pallas_call x1, Pallas kernels: 14.2 us -> 12.4 us  [analysis_call(): pl.pallas_call(analysis_kernel, out_shape=jax.ShapeDtypeStruct((NCELL, n,...]
where the time goes in v4:
time: 149 us
  Pallas kernels  140 us (94%)
  local copies, waits for them, and re-layouts  7.28 us (5%)
    pallas_call x1, Pallas kernels, forecast_call(): pl.pallas_call(functools.partial(forecast_kernel, nm), out_shape=[jax.Sha...  128 us
    pallas_call x1, Pallas kernels, analysis_call(): pl.pallas_call(analysis_kernel, out_shape=jax.ShapeDtypeStruct((NCELL, n,...  12.4 us
    reshape x2, local copies, waits for them, and re-layouts, shards(): x.reshape(mem, nvar, rows * nlon)  3.61 us

profile of v4, /device:TPU:1, one launch (start us, length us, event | category | flops | bytes accessed | tf_op | source)
XLA Modules:
  0.0 148.5 jit_solution(9818686184579038217)
XLA Ops:
  0.7 1.6 %copy.20 = bf16[4,73,6,360]{3,2,1,0:T(8,128)(2,1)S(1)} copy(bf16[4,73,6,360]{3,0,2,1:T(4,128)(2,1)} %param.16) | data formatting | bytes 2522880 | tf_op jit(solution)/shard_map/reshape | solution.py:524
  2.3 2.0 %reshape.8 = bf16[4,73,2160]{2,1,0:T(8,128)(2,1)S(1)} reshape(bf16[4,73,6,360]{3,2,1,0:T(8,128)(2,1)S(1)} %copy.20) | data formatting | bytes 2522880 | tf_op jit(solution)/shard_map/reshape | solution.py:524
  4.3 1.2 pad.4.x_ref
  5.5 128.0 %forecast.1 = (bf16[135,64,128]{2,1,0:T(8,128)(2,1)}, f32[16,8,128]{2,1,0:T(8,128)}) custom-call(bf16[4,80,2304]{2,1,0:T(8,128)(2,1)} %pad.4.x_ref, bf16[6,512,256]{2,1,0:T(8,128)(2,1)} %constant.13.clone.fw_ref, bf16[9,512,256]{2,1,0:T(8,128)(2,1)} %constant.14.clone.iv_ref, bf16[8,96,896]{2,1,0:T(8,128)(2,1)} %constant.15.clone.lf_ref, ...), custom_call_target="tpu_custom_call" | custom-call | tf_op jit(solution)/shard_map/forecast/pallas_call | solution.py:403
  133.5 0.0 copy-start
  133.5 1.6 %copy-done = bf16[135,64,128]{2,1,0:T(8,128)(2,1)S(1)} copy-done((bf16[135,64,128]{2,1,0:T(8,128)(2,1)S(1)}, bf16[135,64,128]{2,1,0:T(8,128)(2,1)}, u32[]{:S(2)}) %copy-start) | copy-done | bytes 2211864
  135.1 0.0 copy-start.1
  135.1 0.8 copy-done.1
  135.9 12.4 %analysis.1 = bf16[135,64,73]{2,1,0:T(8,128)(2,1)} custom-call(f32[16,8,128]{2,1,0:T(8,128)S(1)} %copy-done.1, bf16[135,64,128]{2,1,0:T(8,128)(2,1)S(1)} %copy-done), custom_call_target="tpu_custom_call" | custom-call | tf_op jit(solution)/shard_map/analysis/pallas_call | solution.py:509
Async XLA Ops:
  133.5 1.6 %copy-start = (bf16[135,64,128]{2,1,0:T(8,128)(2,1)S(1)}, bf16[135,64,128]{2,1,0:T(8,128)(2,1)}, u32[]{:S(2)}) copy-start(bf16[135,64,128]{2,1,0:T(8,128)(2,1)} %get-tuple-element.8.field_ref) | copy-start | bytes 6635524
  135.1 0.8 copy-start.1

commit v5 on v4

--- a/solution.py
+++ b/solution.py
@@ -57,18 +57,11 @@
     return lat, chan
 
 
-def window(p):
-    start = 128 * (360 * p // 128)
-    return start, min(512, CELLS - start)
-
-
 def kernel_tables():
     lon_f, lon_i = (np.asarray(a).astype(np.float32) for a in lon_tables(NLON, MMAX))
     lat_f, lat_i = (np.asarray(a).astype(np.float32) for a in lat_tables(NLAT))
-    fw = np.zeros((ROWS, 512, 256), np.float32)
-    for p in range(ROWS):
-        at = 360 * p - window(p)[0]
-        fw[p, at:at + 360, :KCOL] = lon_f
+    fw = np.zeros((NLON, 256), np.float32)
+    fw[:, :KCOL] = lon_f
     iv = np.zeros((9, 2, 256, 256), np.float32)
     for n in range(9):
         low = min(256 * n // 360, 4)
@@ -91,10 +84,10 @@
     return jnp.dot(a, b, preferred_element_type=F32)
 
 
-def forecast_kernel(nm, x_ref, fw_ref, iv_ref, lf_ref, li_ref, sp_ref, gain_ref, lift_ref, w1_ref, w2_ref, ro_ref,
+def forecast_kernel(nm, x_ref, fw_ref, iv_hbm, lf_hbm, li_ref, sp_ref, gain_ref, lift_ref, w1_ref, w2_ref, ro_ref,
                     count_ref, cell_ref, op_ref, val_ref, err_ref,
                     ft_ref, stats_ref,
-                    spec, wmat, acc, bk, fs, field_ref, cp, lx, lt, w1t, w2t, rot, gt, turn, stage, part, got, mid, midg, fin,
+                    spec, wmat, acc, bk, fs, field_ref, cp, lx, lt, w1t, w2t, rot, gt, turn, stage, xk, iv_ref, lf_ref, tab, part, got, mid, midg, fin,
                     ag_s, ag_r, ax_s, ax_r, rs_s, rs_r):
     m, t = lax.axis_index("member"), lax.axis_index("tile")
     nt = 2 * NZ
@@ -110,25 +103,28 @@
         return (m, lax.rem(t + i, nt))
 
     right, left, sib = (m, zat(1) * 2 + core), (m, zat(-1) * 2 + core), (m, z * 2 + 1 - core)
+    tables = [pltpu.make_async_copy(lf_hbm, lf_ref, tab.at[0]), pltpu.make_async_copy(iv_hbm, iv_ref, tab.at[1])]
+    for cc in tables:
+        cc.start()
     bar = pltpu.get_barrier_semaphore()
     for i in range(1, nt):
         pl.semaphore_signal(bar, inc=1, device_id=tile_peer(i), device_id_type=MESH)
     for i in range(1, nm):
         pl.semaphore_signal(bar, inc=1, device_id=member_peer(i), device_id_type=MESH)
 
-    low64 = lax.broadcasted_iota(jnp.int32, (CPAD, 128), 1) < 64
+    low64 = lax.broadcasted_iota(jnp.int32, (VARS, 128), 1) < 64
     low64e = lax.broadcasted_iota(jnp.int32, (EMB, 128), 1) < 64
 
     def half_turn(v):
         return pltpu.roll(v, 64, 1)
+
+    state = [jnp.transpose(x_ref[:, p].astype(F32), (1, 0, 2)) for p in range(ROWS)]
 
     def spectra(pieces):
         tails = {i: [] for i in pieces}
         for p in range(ROWS):
-            at, wide = window(p)
-
             def both(e):
-                v = dot(x_ref[e, :, at:at + wide], fw_ref[p, :wide])
+                v = dot(state[p][e].astype(BF), fw_ref[...])
                 return v[:, :128], v[:, 128:]
 
             for i in pieces:
@@ -149,6 +145,11 @@
             tails[i].append(jnp.zeros((10, 256), F32))
             spec[i, t, 384:CHUNK] = jnp.concatenate(tails[i], axis=0).astype(BF)
 
+    def flatten():
+        for e in range(4):
+            v = jnp.concatenate([state[p][e] for p in range(ROWS)] + [jnp.zeros((VARS, CELLS - ROWS * NLON), F32)], axis=1)
+            xk[e] = jnp.concatenate([v, jnp.zeros((CPAD - VARS, CELLS), F32)], axis=0).astype(BF)
+
     sent = []
 
     def copy(q, dz, other, h, sem, dev):
@@ -222,28 +223,36 @@
         @pl.loop(0, 3)
         def _(it):
             lanes = pl.ds(pl.multiple_of(it * 768, 768), 768)
-            x = x_ref[e, :, lanes]
+            x = xk[e, :, lanes]
             parts = []
             for k in range(3):
                 n = 3 * it + k
                 low = jnp.minimum(256 * n // 360, 4)
                 parts.append(dot(jnp.concatenate([bk[low], bk[low + 1]], axis=1), iv_ref[n]))
             mixed = (jnp.concatenate(parts, axis=1) + dot(lt[...], x)).astype(BF)
-            u = dot(w1t[...], mixed)
+            u = dot(w1t[...], mixed).astype(BF)
             h = 0.5 * u
             u = h * jnp.tanh(u * (c0 + (c0 * 0.044715) * (u * u))) + h
-            outer = (mixed.astype(F32) + dot(w2t[...], u.astype(BF))).astype(BF)
+            outer = (mixed.astype(F32) + dot(w2t[...], u)).astype(BF)
             fs[e, :, lanes] = (x.astype(F32) + dot(rot[...], outer)).astype(BF)
-
-        for i in range(1, nm):
-            go(out_copy(e, i))
+            for k in range(6):
+                to = 6 * it - 1 + k
+
+                @pl.when((to >= 0) & (to < nm) & (to != m))
+                def _():
+                    out_copy(e, to).start()
+
         field_ref[nm * e + m] = fs[e, :, pl.ds(pl.multiple_of(128 * m, 128), 256)]
 
-    def out_copy(e, i):
-        to = lax.rem(m + i, nm)
+    def out_copy(e, to):
         return pltpu.make_async_remote_copy(
             src_ref=fs.at[e, :, pl.ds(pl.multiple_of(128 * to, 128), 256)], dst_ref=field_ref.at[nm * e + m],
-            send_sem=ax_s.at[e, i], recv_sem=ax_r.at[e, i], device_id=(to, t), device_id_type=MESH)
+            send_sem=ax_s.at[e, to], recv_sem=ax_r.at[e, m], device_id=(to, t), device_id_type=MESH)
+
+    def in_copy(e, src):
+        return pltpu.make_async_remote_copy(
+            src_ref=fs.at[e, :, pl.ds(0, 256)], dst_ref=field_ref.at[nm * e + src],
+            send_sem=ax_s.at[e, src], recv_sem=ax_r.at[e, src], device_id=(src, t), device_id_type=MESH)
 
     spectra((0,))
     pl.semaphore_wait(bar, nt + nm - 2)
@@ -255,6 +264,7 @@
     lt[...] = lv
     lx[...] = dot(lv[:, :VARS], sp_ref[...]).astype(BF)
     gt[...] = gain_ref[...].T
+    tables[0].wait()
     weights(1)
     weights(-1)
     weights(2)
@@ -262,6 +272,8 @@
     step(0, 1)
     weights(3)
     step(1, 1)
+    flatten()
+    tables[1].wait()
     weights(-3)
     weights(0)
     from_sib(0, 1)
@@ -309,8 +321,8 @@
     from_sib(2, 2)
     from_sib(2, -2)
     apply(2, 2, -2)
+    member(1)
     step(2, 4)
-    member(1)
     from_sib(2, 3)
     from_sib(2, -3)
     apply(2, 3, -3)
@@ -342,9 +354,10 @@
 
     def collect(e):
         for i in range(nm):
+            src = lax.rem(m - i + nm, nm)
             if i:
-                out_copy(e, i).wait_recv()
-            counterparts(e, lax.rem(m - i + nm, nm))
+                in_copy(e, src).wait_recv()
+            counterparts(e, src)
 
     for e in range(3):
         collect(e)
@@ -352,6 +365,9 @@
     for cc in sent:
         cc.wait_send()
     sent.clear()
+    for e in range(4):
+        for i in range(1, nm):
+            out_copy(e, lax.rem(m + i, nm)).wait_send()
     collect(3)
     c = cp[...]
     n = c.shape[0]
@@ -403,7 +419,7 @@
     return pl.pallas_call(
         functools.partial(forecast_kernel, nm),
         out_shape=[jax.ShapeDtypeStruct((NCELL, n, 128), BF), jax.ShapeDtypeStruct((nt, 8, 128), F32)],
-        in_specs=[vm] * len(args),
+        in_specs=[pl.BlockSpec(memory_space=pl.ANY) if i in (2, 3) else vm for i in range(len(args))],
         out_specs=[vm, vm],
         scratch_shapes=[
             pltpu.VMEM((3, nt, CHUNK, 256), BF),
@@ -421,6 +437,10 @@
             pltpu.VMEM((EMB, NLAT), F32),
             pltpu.VMEM((16, 256, 128), F32),
             pltpu.VMEM((NCELL, 16, 128), F32),
+            pltpu.VMEM((4, CPAD, CELLS), BF),
+            pltpu.VMEM((9, 512, 256), BF),
+            pltpu.VMEM((NZ, NLAT, 2 * CHUNK), BF),
+            dma((2,)),
             pltpu.VMEM((nt, 8, 128), F32),
             pltpu.VMEM((nt, 8, 128), F32),
             pltpu.VMEM((8, 128), F32),
@@ -512,7 +532,7 @@
         in_specs=[vm, pl.BlockSpec(memory_space=pl.ANY)],
         out_specs=vm,
         scratch_shapes=[pltpu.VMEM((NCELL, n, 128), BF), pltpu.SemaphoreType.DMA],
-        compiler_params=pltpu.CompilerParams(vmem_limit_bytes=40 * 2**20),
+        compiler_params=pltpu.CompilerParams(vmem_limit_bytes=60 * 2**20),
         name="analysis",
     )(stats, ft)
 
@@ -521,8 +541,7 @@
     mem, nvar, rows, nlon = x.shape
     nt, nm = lax.axis_size("tile"), lax.axis_size("member")
     tables = (jnp.asarray(a) for a in kernel_tables())
-    xk = jnp.pad(x.reshape(mem, nvar, rows * nlon), ((0, 0), (0, CPAD - nvar), (0, CELLS - rows * nlon)))
-    args = (xk, *tables, gain.T, lift, w1, w2, readout.T,
+    args = (jnp.transpose(x, (1, 2, 0, 3)), *tables, gain.T, lift, w1, w2, readout.T,
             obs_count.reshape(1, 1), obs_cell, obs_op.transpose(2, 0, 1), obs_value, obs_error)
     ft, stats = forecast_call(args, nm, nt, mem * nm)
     return jnp.transpose(analysis_call(stats, ft), (2, 0, 1))

time: 149 us -> 139 us (0.933)
  local copies, waits for them, and re-layouts: 7.28 us -> 0 us
  Pallas kernels: 140 us -> 138 us
    reshape x2 -> x0, local copies, waits for them, and re-layouts: 3.61 us -> none  [shards(): x.reshape(mem, nvar, rows * nlon)]
    unnamed x4 -> x0, local copies, waits for them, and re-layouts: 2.46 us -> none
    pallas_call x1, Pallas kernels: 128 us -> 126 us  [forecast_call(): pl.pallas_call(functools.partial(forecast_kernel, nm), out_shape=[jax.Sha...]
where the time goes in v5:
time: 139 us
  Pallas kernels  138 us (99%)
    pallas_call x1, Pallas kernels, forecast_call(): pl.pallas_call(functools.partial(forecast_kernel, nm), out_shape=[jax.Sha...  126 us
    pallas_call x1, Pallas kernels, analysis_call(): pl.pallas_call(analysis_kernel, out_shape=jax.ShapeDtypeStruct((NCELL, n,...  12.8 us

profile of v5, /device:TPU:1, one launch (start us, length us, event | category | flops | bytes accessed | tf_op | source)
XLA Modules:
  0.0 139.2 jit_solution(5282586435230897673)
XLA Ops:
  0.7 125.6 %forecast.1 = (bf16[135,64,128]{2,1,0:T(8,128)(2,1)}, f32[16,8,128]{2,1,0:T(8,128)}) custom-call(bf16[73,6,4,360]{3,2,1,0:T(4,128)(2,1)} %bitcast.7, bf16[360,256]{1,0:T(8,128)(2,1)} %constant.10.clone.fw_ref, bf16[9,512,256]{2,1,0:T(8,128)(2,1)} %constant.11.clone.iv_hbm, bf16[8,96,896]{2,1,0:T(8,128)(2,1)} %constant.12.clone.lf_hbm, ...), custom_call_target="tpu_custom_call" | custom-call | tf_op jit(solution)/shard_map/forecast/pallas_call | solution.py:419
  126.3 12.8 %analysis.1 = bf16[135,64,73]{2,1,0:T(8,128)(2,1)} custom-call(f32[16,8,128]{2,1,0:T(8,128)} %get-tuple-element.7.stats_ref, bf16[135,64,128]{2,1,0:T(8,128)(2,1)} %get-tuple-element.8.field_ref), custom_call_target="tpu_custom_call" | custom-call | tf_op jit(solution)/shard_map/analysis/pallas_call | solution.py:529
